TPU v7x, 256 devices: a whole 4x4x8 slice. The times are simulated.
256 devices in a mesh: lon: 32 (over y_hi, z, core), lat: 8 (over y_lo, x).
Axes of the slice: x: 4, y: 4 (y_hi: 2, y_lo: 2; y = y_hi * 2 + y_lo), z: 8, core: 2. Of those that a mesh axis runs over, the one named last changes fastest.
Arguments:
- layer_u: float32 [12, 512, 4096], P(None, 'lat', 'lon'), may hold values from -3 to 3
- layer_v: float32 [12, 512, 4096], P(None, 'lat', 'lon'), may hold values from -3 to 3
- thickness: float32 [12, 512, 4096], P(None, 'lat', 'lon'), may hold values from 0.02 to 0.16
- surface_height: float32 [512, 4096], P('lat', 'lon'), may hold values from -2 to 2
- barotropic_u: float32 [512, 4096], P('lat', 'lon'), may hold values from -2 to 2
- barotropic_v: float32 [512, 4096], P('lat', 'lon'), may hold values from -2 to 2
- land_mask: int32 [512, 4096], P('lat', 'lon'), may hold values 0 or 1
- bottom_level: int32 [512, 4096], P('lat', 'lon'), may hold values from 1 to 12
- fold_map: int32 [4096], P('lon'), may hold values from 0 to 4095, as said below
- reduced_gravity: float32 [12], replicated, may hold values from 0.05 to 0.5
Outputs:
- new_u: float32 [12, 512, 4096], P(None, 'lat', 'lon')
- new_v: float32 [12, 512, 4096], P(None, 'lat', 'lon')
- new_thickness: float32 [12, 512, 4096], P(None, 'lat', 'lon')
- new_surface: float32 [512, 4096], P('lat', 'lon')
- mean_u: float32 [512, 4096], P('lat', 'lon')
- mean_v: float32 [512, 4096], P('lat', 'lon')
Inputs may be any that keep to these rules, and one draw needn't show every extreme that they name: fold_map[i] = (p - i) mod 4096 for one p, so the map is its own inverse.
All inputs are finite; a program needn't handle non-finite values. No bound on the sum of `land_mask` on one device may be relied on, other than what follows from the above.
Results may differ from a plain program's by a relative error of at most 0.00002.
Values sent between devices are 32-bit elements; how exact they have to be, the bound alone decides.
No kernel may reach another device: no remote copies, remote signals or barrier semaphores. Data moves between devices by JAX's collectives and lax.ppermute only.
A program may use at most 64 MiB of HBM per device.

v0:
```python
import jax
import jax.numpy as jnp
from jax import lax
from jax.experimental import pallas as pl
from jax.experimental.pallas import tpu as pltpu
from jax.sharding import PartitionSpec as P

SUBSTEPS = 8
LAYERS = 12
TOTAL_ROWS = 512
ROWS, COLS = 64, 128
HALO = 16

barotropic_step = 0.45
baroclinic_step = 0.1
coriolis_scale = 0.3
bottom_drag = 0.05

PAIR_LANE, EAST_PAIR_LANE = 96, 80
PAIR_END = PAIR_LANE + 2 * LAYERS
TOP_ROW, W_TOP, C_TOP, V_TOP, W_BOTTOM, LON_ROWS = 64, 112, 124, 136, 137, 152
V_BOTTOM = LAYERS
LAT_W, LAT_C, LAT_V, LAT_SIDE, LAT_ROWS = 96, 108, 120, 128, 160
FULL = ROWS + 2 * HALO
WIDE = 2 * COLS
half = 0.5 * baroclinic_step


def lane_index(shape):
    return lax.broadcasted_iota(jnp.int32, shape, 1)


def row_index(shape):
    return lax.broadcasted_iota(jnp.int32, shape, 0)


def roll(x, shift, axis):
    shift = shift % x.shape[axis]
    return x if shift == 0 else pltpu.roll(x, shift, axis)


def first_kernel(
    gravity_hbm, lu_hbm, lv_hbm, th_hbm, lev_hbm, u_hbm, v_hbm, land_hbm, bottom_hbm, fold_hbm,
    msg_a, msg_b, own_pairs, own_rows, flat, cor_out, g_rows, tail_u, tail_v, weight, th, floor,
    lu, lv, gravity, fold, sems,
):
    pairs = (
        (th_hbm, th), (land_hbm, floor.at[0]), (bottom_hbm, floor.at[1]), (gravity_hbm, gravity), (lu_hbm, lu),
        (lv_hbm, lv), (lev_hbm, flat.at[5]), (u_hbm, flat.at[6]), (v_hbm, flat.at[7]),
        (fold_hbm, fold),
    )
    copies = [pltpu.make_async_copy(a, b, sems.at[n]) for n, (a, b) in enumerate(pairs)]
    for copy in copies:
        copy.start()
    lon, lat = lax.axis_index("lon"), lax.axis_index("lat")
    even = lax.rem(lon, 2) == 0
    rows = (row_index((FULL, COLS)) + (lat * ROWS - HALO)).astype(jnp.float32)
    cor_all = -coriolis_scale * jnp.cos((rows + 0.5) * (jnp.pi / TOTAL_ROWS))
    cor_out[...] = cor_all
    cor = cor_all[HALO : HALO + ROWS]
    lane = lane_index((ROWS, COLS))
    row = row_index((ROWS, COLS))
    for copy in copies:
        copy.wait()
    wet = floor[0].astype(jnp.float32)
    bot = floor[1]
    lev, u, v = flat[5], flat[6], flat[7]
    zero = jnp.zeros((ROWS, COLS), jnp.float32)
    line = lane_index((1, COLS))
    lanes_g = jnp.zeros((1, COLS), jnp.float32)
    for k in range(LAYERS):
        g_rows[k : k + 1, :] = jnp.full((1, COLS), gravity[k], jnp.float32)
        lanes_g = jnp.where((line - PAIR_LANE) >> 1 == k, gravity[k], lanes_g)
    g_rows[LAYERS : LAYERS + 1, :] = lanes_g
    offset = 64 + ((fold[0] + 64) & (COLS - 1))
    g_rows[LAYERS + 1 : LAYERS + 2, :] = jnp.full((1, COLS), offset, jnp.int32).astype(jnp.float32)
    lons = lax.axis_size("lon")
    apart = lax.rem((fold[0] + lons * COLS - 64) // COLS - lon + lons, lons)
    g_rows[LAYERS + 2 : LAYERS + 3, :] = jnp.full((1, COLS), jnp.where(apart == 0, 1.0, 0.0), jnp.float32)
    g_rows[LAYERS + 3 :, :] = jnp.zeros((1, COLS), jnp.float32)

    depth, potential = zero, zero
    grad_u, grad_v, sum_u, sum_v = zero, zero, zero, zero
    for k in range(LAYERS):
        w = jnp.where(bot > k, wet, 0.0) * th[k]
        depth = depth + w
        potential = potential + gravity[k] * depth
        right = jnp.where(lane == COLS - 1, 0.0, roll(potential, -1, 1))
        left = jnp.where(lane == 0, 0.0, roll(potential, 1, 1))
        above = jnp.where(row == ROWS - 1, 0.0, roll(potential, -1, 0))
        below = jnp.where(row == 0, 0.0, roll(potential, 1, 0))
        du = 0.5 * (left - right)
        dv = 0.5 * (below - above)
        grad_u = grad_u + w * du
        grad_v = grad_v + w * dv
        sum_u = sum_u + w * lu[k]
        sum_v = sum_v + w * lv[k]
        rest_u = lu[k] + baroclinic_step * (du + cor * lv[k])
        rest_v = lv[k] + baroclinic_step * (dv - cor * lu[k])
        tail_u[k] = rest_u
        tail_v[k] = rest_v
        weight[k] = w
        for msg in (msg_a, msg_b):
            msg[W_TOP + k : W_TOP + k + 1, :] = w[ROWS - 1 :]
            msg[W_BOTTOM + k : W_BOTTOM + k + 1, :] = w[:1]
            msg[C_TOP + k : C_TOP + k + 1, :] = rest_v[ROWS - 1 :]
        own_rows[k : k + 1, :] = rest_v[:1]
    edge_w, edge_c = zero, zero
    for k in range(LAYERS):
        here = lane >> 1 == k
        edge_w = jnp.where(here, roll(weight[k], 2 * k + 1, 1), edge_w)
        edge_c = jnp.where(here, roll(tail_u[k], 2 * k + 1, 1), edge_c)
    own_pairs[...] = edge_w
    inverse = 1.0 / (depth + (1.0 - wet))
    column_u = sum_u * inverse
    column_v = sum_v * inverse
    force_u = grad_u * inverse + cor * column_v
    force_v = grad_v * inverse - cor * column_u
    fields = (depth, u, v, lev, force_u, force_v)
    flat[0] = depth
    flat[1] = force_u
    flat[2] = force_v
    flat[3] = column_u
    flat[4] = column_v
    transport_u = depth * u
    transport_v = depth * v
    is_odd = lane % 2 == 1
    west, east = zero, zero
    for f, field in enumerate(fields):
        moved = roll(field, HALO * f, 1)
        west = jnp.where(lane // HALO == f, moved, west)
        east = jnp.where(lane // HALO == (f - 1) % 8, moved, east)
    in_west = (lane >= PAIR_LANE) & (lane < PAIR_END)
    in_east = (lane >= EAST_PAIR_LANE) & (lane < EAST_PAIR_LANE + 2 * LAYERS)

    def pairs_of(w, rest, edge):
        column = jnp.sum(jnp.where(lane == edge, column_u, 0.0), axis=1, keepdims=True)
        return jnp.where(is_odd, rest - column, w)

    west = jnp.where(in_west, pairs_of(roll(edge_w, PAIR_LANE - 1, 1), roll(edge_c, PAIR_LANE, 1), 0), west)
    west = jnp.where(lane == PAIR_END, roll(transport_u, PAIR_END - HALO, 1), west)
    at = EAST_PAIR_LANE
    east = jnp.where(in_east, pairs_of(roll(edge_w, at, 1), roll(edge_c, at + 1, 1), COLS - 1), east)
    at = PAIR_END - HALO
    east = jnp.where(lane == at, roll(transport_u, at - (COLS - 1 - HALO), 1), east)
    msg_a[:ROWS] = jnp.where(even, east, west)
    msg_b[:ROWS] = jnp.where(even, west, east)
    low = lane_index((8, COLS)) < 64
    for f, field in enumerate(fields):
        lower, upper = field[ROWS - HALO : ROWS - 8], field[ROWS - 8 :]
        west = jnp.where(low, roll(lower, -16, 1), roll(upper, 48, 1))
        east = jnp.where(low, roll(lower, -48, 1), roll(upper, 16, 1))
        msg_a[TOP_ROW + 8 * f : TOP_ROW + 8 * (f + 1)] = jnp.where(even, east, west)
        msg_b[TOP_ROW + 8 * f : TOP_ROW + 8 * (f + 1)] = jnp.where(even, west, east)
    for msg in (msg_a, msg_b):
        msg[C_TOP : C_TOP + LAYERS] = msg[C_TOP : C_TOP + LAYERS] - column_v[ROWS - 1 :]
        msg[V_TOP : V_TOP + 1] = transport_v[ROWS - 1 - HALO : ROWS - HALO]
        msg[W_BOTTOM + LAYERS :] = jnp.zeros((LON_ROWS - W_BOTTOM - LAYERS, COLS), jnp.float32)
    own_rows[:LAYERS] = own_rows[:LAYERS] - column_v[:1]
    own_rows[V_BOTTOM : V_BOTTOM + 1] = transport_v[HALO : HALO + 1]
    own_rows[V_BOTTOM + 1 :] = jnp.zeros((16 - V_BOTTOM - 1, COLS), jnp.float32)


def lane_prefix(x):
    for shift in (2, 4, 8, 16):
        x = x + pltpu.roll(x, shift, 1)
    return x


def second_kernel(g_rows, flat, own_pairs, own_rows, own_a, got_a, got_b, ext, edges, msg_x, msg_y, msg_f):
    lon, lat = lax.axis_index("lon"), lax.axis_index("lat")
    even_lon = lax.rem(lon, 2) == 0
    even_lat = lax.rem(lat, 2) == 0
    lane = lane_index((ROWS, COLS))
    is_pair = (lane >= PAIR_LANE) & (lane < PAIR_END)
    is_odd = lane % 2 == 1
    sign = jnp.where(is_odd, -1.0, 1.0)
    weights_g = g_rows[LAYERS : LAYERS + 1, :]
    east = jnp.where(even_lon, got_a[:ROWS], got_b[:ROWS])
    west = jnp.where(even_lon, got_b[:ROWS], got_a[:ROWS])

    def potentials(w):
        return lane_prefix(weights_g * lane_prefix(w))

    def dots(x):
        even_sum = jnp.sum(jnp.where(is_odd, 0.0, x), axis=1, keepdims=True)
        odd_sum = jnp.sum(jnp.where(is_odd, x, 0.0), axis=1, keepdims=True)
        return 0.5 * even_sum, 0.5 * odd_sum

    apart = PAIR_LANE - EAST_PAIR_LANE
    w_halo = jnp.where(is_pair, jnp.where(is_odd, roll(west, apart + 1, 1), east), 0.0)
    c_halo = jnp.where(is_odd, roll(west, apart, 1), roll(east, -1, 1))
    w_own = roll(own_pairs[...], PAIR_LANE, 1)
    p_halo, p_own = potentials(w_halo), potentials(w_own)
    edges[0] = (-half * sign) * p_halo
    edges[1] = w_halo * (c_halo + (half * sign) * p_own)
    edges[2] = w_halo

    depth = flat[0]
    safe = depth + jnp.where(depth > 0.0, 0.0, 1.0)
    to_e, to_w = dots(w_own * p_halo)
    force_u = flat[1] + jnp.where(lane == COLS - 1, -to_e, jnp.where(lane == 0, to_w, 0.0)) / safe

    sides = [roll(jnp.where(lane // HALO == f, east, west), -HALO * f, 1) for f in range(6)]
    sides[1] = jnp.where(lane == HALO, roll(east, HALO - PAIR_END, 1), sides[1])
    at = COLS - HALO - 1
    sides[1] = jnp.where(lane == at, roll(west, at - (PAIR_END - HALO), 1), sides[1])
    safe = sides[0] + jnp.where(sides[0] > 0.0, 0.0, 1.0)
    to_e, to_w = dots(w_halo * p_own)
    sides[4] = sides[4] + jnp.where(lane == 0, to_e, jnp.where(lane == COLS - 1, -to_w, 0.0)) / safe
    sides[0] = jnp.where((lane == HALO) | (lane == at), 1.0, sides[0])

    for f, field in enumerate((depth, flat[6], flat[7], flat[5], force_u, flat[2])):
        ext[f, :, :COLS] = field
        ext[f, :, COLS:] = sides[f]

    lane12 = lane_index((LAYERS, COLS))
    lane16 = lane_index((HALO, COLS))

    def lat_message(msg, north):
        start, w_at = (ROWS - HALO, W_TOP) if north else (0, W_BOTTOM)
        edge, c_at, v_at = (own_a, C_TOP, V_TOP) if north else (own_rows, 0, V_BOTTOM)
        packed = [jnp.zeros((HALO, COLS), jnp.float32)] * 2
        for f in range(6):
            msg[HALO * f : HALO * (f + 1), :] = ext[f, start : start + HALO, :COLS]
            side = roll(ext[f, start : start + HALO, COLS:], HALO + 32 * (f % 4), 1)
            packed[f // 4] = jnp.where(lane16 // 32 == f % 4, side, packed[f // 4])
        msg[LAT_SIDE : LAT_SIDE + HALO, :] = packed[0]
        msg[LAT_SIDE + HALO :, :] = packed[1]
        msg[LAT_W : LAT_W + LAYERS, :] = own_a[w_at : w_at + LAYERS, :]
        beside_e = jnp.where(even_lon, got_a[w_at : w_at + LAYERS, :], got_b[w_at : w_at + LAYERS, :])
        beside_w = jnp.where(even_lon, got_b[w_at : w_at + LAYERS, :], got_a[w_at : w_at + LAYERS, :])
        beside = roll(jnp.where(lane12 < HALO, beside_e, beside_w), HALO + 64, 1)
        held = msg[LAT_SIDE + HALO : LAT_SIDE + HALO + LAYERS, :]
        msg[LAT_SIDE + HALO : LAT_SIDE + HALO + LAYERS, :] = jnp.where(lane12 // 32 == 2, beside, held)
        msg[LAT_C : LAT_C + LAYERS, :] = edge[c_at : c_at + LAYERS, :]
        msg[LAT_V : LAT_V + 1, :] = edge[v_at : v_at + 1, :]
        msg[LAT_V + 1 : LAT_SIDE, :] = jnp.zeros((LAT_SIDE - LAT_V - 1, COLS), jnp.float32)

    @pl.when(even_lat)
    def _():
        lat_message(msg_x, True)
        lat_message(msg_y, False)

    @pl.when(jnp.logical_not(even_lat))
    def _():
        lat_message(msg_x, False)
        lat_message(msg_y, True)

    @pl.when(lat == lax.axis_size("lat") - 1)
    def _():
        lane8 = lane_index((8, COLS))
        row8 = row_index((8, COLS))
        offset = jnp.broadcast_to(g_rows[LAYERS + 1 : LAYERS + 2, :].astype(jnp.int32), (8, COLS))
        source = (offset - lane8) & (COLS - 1)
        block = (COLS + offset - lane8) >> 7
        side_block = jnp.where(lane8 < HALO, offset - lane8, 2 * COLS + offset - lane8) >> 7

        def gather(x, index, axis):
            return jnp.take_along_axis(x, index, axis=axis, mode="promise_in_bounds")

        def window(w_tile, o_tile, e_tile):
            a, b, c = gather(w_tile, source, 1), gather(o_tile, source, 1), gather(e_tile, source, 1)
            main = jnp.where(block == 0, a, jnp.where(block == 1, b, c))
            side = jnp.where(side_block == 0, a, jnp.where(side_block == 1, b, c))
            return main, side

        def tiles(at):
            on_e = jnp.where(even_lon, got_a[at : at + 8, :], got_b[at : at + 8, :])
            on_w = jnp.where(even_lon, got_b[at : at + 8, :], got_a[at : at + 8, :])
            return on_w, own_a[at : at + 8, :], on_e

        packed = {}

        def pack(at, group, x):
            x = roll(x, HALO + 32 * group, 1)
            packed[at] = jnp.where(lane8 // 32 == group, x, packed[at]) if at in packed else x

        for f in range(6):
            sign = 1.0 if f in (0, 3) else -1.0
            for t in range(2):
                at = ROWS - 8 * (t + 1)
                mine = ext[f, at : at + 8, :COLS]
                side = ext[f, at : at + 8, COLS:]
                on_w, _, on_e = tiles(TOP_ROW + 8 * f)
                on_e = jnp.where(lane8 < HALO, side, roll(on_e, -48 if t == 0 else 16, 1))
                on_w = jnp.where(lane8 >= COLS - HALO, side, roll(on_w, -16 if t == 0 else 48, 1))
                main, beside = window(on_w, mine, on_e)
                msg_f[HALO * f + 8 * t : HALO * f + 8 * (t + 1), :] = sign * gather(main, 7 - row8, 0)
                pack(LAT_SIDE + HALO * (f // 4) + 8 * t, f % 4, sign * gather(beside, 7 - row8, 0))
        for t in range(3):
            main, beside = window(*tiles(W_TOP + 8 * t))
            sign = jnp.where(row8 + 8 * t < LAYERS, 1.0, -1.0)
            msg_f[LAT_W + 8 * t : LAT_W + 8 * (t + 1), :] = sign * main
            if t < 2:
                pack(LAT_SIDE + HALO + 8 * t, 2, beside)
        main, _ = window(*tiles(V_TOP))
        msg_f[LAT_V : LAT_V + 8, :] = -main
        for at, x in packed.items():
            msg_f[at : at + 8, :] = x

    @pl.when(lat != lax.axis_size("lat") - 1)
    def _():
        msg_f[...] = msg_y[...]


def third_kernel(
    g_rows, tail_u, tail_v, weight, th, floor, flat, cor_ref, edges, ext, own_x, own_y, own_f, got_x, got_f_hbm,
    new_u_hbm, new_v_hbm, new_th_hbm, new_lev_hbm, mean_u_hbm, mean_v_hbm,
    far, level_pad, v_pad, state, fixed, pots, seam_w, seam_rows, new_u, new_v, new_th, planes,
    sems, plane_sems, far_sem,
):
    lat = lax.axis_index("lat")
    even = lax.rem(lat, 2) == 0
    at_top = lat == lax.axis_size("lat") - 1
    at_bottom = lat == 0

    fold_copy = pltpu.make_async_copy(got_f_hbm, far, far_sem.at[0])
    fold_copy.start()
    inner = slice(HALO, HALO + ROWS)

    def place(at, count, depth, u, v, level, force_u, force_v, rate):
        rows = pl.ds(at, count)
        cor = cor_ref[rows, :]
        cor = jnp.concatenate([cor, cor], axis=1)
        wet = jnp.where(depth > 0.0, 1.0, 0.0)
        fixed[0, rows, :] = depth
        fixed[1, rows, :] = wet * (1.0 - barotropic_step * bottom_drag)
        fixed[2, rows, :] = wet * (barotropic_step * cor)
        fixed[3, rows, :] = wet * (barotropic_step * force_u)
        fixed[4, rows, :] = wet * (barotropic_step * force_v)
        fixed[5, rows, :] = wet * (0.5 * barotropic_step)
        fixed[6, rows, :] = jnp.full((count, WIDE), rate, jnp.float32)
        state[0, rows, :] = u
        state[1, rows, :] = v
        level_pad[pl.ds(at + 8, count), :] = level

    place(HALO, ROWS, *(ext[f] for f in range(6)), 0.5 * barotropic_step)

    def strip(got, mine, slot, is_north, keep):
        at = pl.multiple_of(jnp.where(is_north, HALO + ROWS, 0), HALO)
        sign = jnp.where(is_north, 1.0, -1.0)
        fields = []
        for f in range(6):
            main = got[HALO * f : HALO * (f + 1), :]
            side = got[LAT_SIDE + HALO * (f // 4) : LAT_SIDE + HALO * (f // 4 + 1), :]
            side = roll(side, -HALO - 32 * (f % 4), 1)
            fields.append(jnp.concatenate([main, side], axis=1))
        if keep is not None:
            fields = [jnp.where(keep, field, 0.0) for field in fields]
        rate = 0.5 * barotropic_step
        place(at, HALO, *fields, rate if keep is None else jnp.where(keep, rate, 0.0))
        v_row = got[LAT_V : LAT_V + 1, :]
        if keep is not None:
            v_row = jnp.where(keep, v_row, 0.0)
        v_rows = pl.ds(pl.multiple_of(jnp.where(is_north, 8 + FULL, 0), 8), 8)
        v_pad[v_rows, :COLS] = jnp.broadcast_to(v_row, (8, COLS))
        v_pad[v_rows, COLS:] = jnp.zeros((8, COLS), jnp.float32)
        for n, ref in enumerate((mine, got)):
            w = ref[LAT_W : LAT_W + LAYERS, :]
            side = roll(ref[LAT_SIDE + HALO : LAT_SIDE + HALO + LAYERS, :], -HALO - 64, 1)
            if n == 1 and keep is not None:
                w, side = jnp.where(keep, w, 0.0), jnp.where(keep, side, 0.0)
            seam_w[n, :LAYERS, :COLS] = w
            seam_w[n, :LAYERS, COLS:] = side
        sum_o, sum_s, pot_o, pot_s, to_o, to_s = (jnp.zeros((1, WIDE), jnp.float32) for _ in range(6))
        for k in range(LAYERS):
            wo, ws = seam_w[0, k : k + 1, :], seam_w[1, k : k + 1, :]
            g = jnp.concatenate([g_rows[k : k + 1, :]] * 2, axis=1)
            sum_o, sum_s = sum_o + wo, sum_s + ws
            pot_o, pot_s = pot_o + g * sum_o, pot_s + g * sum_s
            to_o = to_o + wo * pot_s
            to_s = to_s + ws * pot_o
            pots[0, k : k + 1, :] = pot_o[:, :COLS]
            pots[1, k : k + 1, :] = pot_s[:, :COLS]
        safe_o = sum_o + jnp.where(sum_o > 0.0, 0.0, 1.0)
        safe_s = sum_s + jnp.where(sum_s > 0.0, 0.0, 1.0)
        scale = 0.5 * barotropic_step * sign
        row8 = row_index((8, WIDE))
        own_rows = pl.ds(pl.multiple_of(jnp.where(is_north, HALO + ROWS - 8, HALO), 8), 8)
        strip_rows = pl.ds(pl.multiple_of(jnp.where(is_north, HALO + ROWS, HALO - 8), 8), 8)
        last, first = row8 == jnp.where(is_north, 7, 0), row8 == jnp.where(is_north, 0, 7)
        fixed[4, own_rows, :] = fixed[4, own_rows, :] - jnp.where(last, scale * to_o / safe_o, 0.0)
        fixed[4, strip_rows, :] = fixed[4, strip_rows, :] + jnp.where(first, scale * to_s / safe_s, 0.0)
        side = jnp.where(is_north, 0, 3)
        w = seam_w[1, :LAYERS, :COLS]
        seam_rows[side, :LAYERS, :] = (-half * sign) * pots[1, :LAYERS, :]
        seam_rows[side + 1, :LAYERS, :] = w * (got[LAT_C : LAT_C + LAYERS, :] + (half * sign) * pots[0, :LAYERS, :])
        seam_rows[side + 2, :LAYERS, :] = w

    strip(got_x, own_x, 0, even, None)
    fold_copy.wait()

    far[...] = jnp.where(at_top & (g_rows[LAYERS + 2 : LAYERS + 3, :] > 0.0), own_f[...], far[...])
    strip(far, own_y, 1, jnp.logical_not(even), jnp.logical_not(at_bottom))

    for step in range(SUBSTEPS):
        depth, u, v = fixed[0], state[0], state[1]
        trans_u = depth * u
        v_pad[8 : 8 + FULL, :] = depth * v
        dv = v_pad[9 : 9 + FULL, :] - v_pad[7 : 7 + FULL, :]
        du = pltpu.roll(trans_u, WIDE - 1, 1) - pltpu.roll(trans_u, 1, 1)
        level = level_pad[8 : 8 + FULL, :] - fixed[6] * (du + dv)
        level_pad[8 : 8 + FULL, :] = level
        dy = level_pad[9 : 9 + FULL, :] - level_pad[7 : 7 + FULL, :]
        dx = pltpu.roll(level, WIDE - 1, 1) - pltpu.roll(level, 1, 1)
        keep, turn, slope = fixed[1], fixed[2], fixed[5]
        next_u = keep * u + turn * v + fixed[3] - slope * dx
        next_v = keep * v - turn * u + fixed[4] - slope * dy
        state[0] = next_u
        state[1] = next_v
        state[2] = next_u if step == 0 else state[2] + next_u
        state[3] = next_v if step == 0 else state[3] + next_v
    planes[0] = level_pad[8 + HALO : 8 + HALO + ROWS, :COLS]
    planes[1] = state[2, inner, :COLS] * (1.0 / SUBSTEPS)
    planes[2] = state[3, inner, :COLS] * (1.0 / SUBSTEPS)
    plane_copies = [
        pltpu.make_async_copy(planes.at[n], out, plane_sems.at[n])
        for n, out in enumerate((new_lev_hbm, mean_u_hbm, mean_v_hbm))
    ]
    for copy in plane_copies:
        copy.start()

    to_force = baroclinic_step / barotropic_step

    def rest(n, rows, lanes):
        return state[2 + n, rows, lanes] * (1.0 / SUBSTEPS) - to_force * fixed[3 + n, rows, lanes]

    main, beside = slice(0, COLS), slice(COLS, WIDE)
    lane = lane_index((ROWS, COLS))
    row = row_index((ROWS, COLS))
    is_e, is_w = lane == COLS - 1, lane == 0
    is_n, is_s = row == ROWS - 1, row == 0
    is_edge = is_e | is_w
    base_u = rest(0, inner, main) - flat[3]
    base_v = rest(1, inner, main) - flat[4]
    side_u = rest(0, inner, beside)
    rest_e = jnp.sum(jnp.where(is_w, side_u, 0.0), axis=1, keepdims=True)
    rest_w = jnp.sum(jnp.where(is_e, side_u, 0.0), axis=1, keepdims=True)
    pair_flux = edges[1] + edges[2] * jnp.where(lane % 2 == 0, rest_e, rest_w)
    pair_fix = edges[0]
    rest_n = rest(1, slice(HALO + ROWS, HALO + ROWS + 1), main)
    rest_s = rest(1, slice(HALO - 1, HALO), main)
    for side, line in ((0, rest_n), (3, rest_s)):
        seam_rows[side + 1, :LAYERS, :] = seam_rows[side + 1, :LAYERS, :] + seam_rows[side + 2, :LAYERS, :] * line
    levels = jnp.where(floor[0] > 0, floor[1], 0)
    copies = []
    parts = ((0, 4), (4, 8), (8, 11), (11, 12))
    for k in range(LAYERS):
        w = weight[k]
        mask = levels > k
        shift = COLS - 1 - PAIR_LANE - 2 * k
        fix_u = jnp.where(is_edge, roll(pair_fix, shift, 1), 0.0)
        fix_v = jnp.where(is_n, seam_rows[0, k : k + 1, :], jnp.where(is_s, seam_rows[3, k : k + 1, :], 0.0))
        out_u = jnp.where(mask, tail_u[k] + base_u + fix_u, 0.0)
        out_v = jnp.where(mask, tail_v[k] + base_v + fix_v, 0.0)
        new_u[k] = out_u
        new_v[k] = out_v
        flux_u, flux_v = w * out_u, w * out_v
        halo = roll(pair_flux, shift, 1)
        east = jnp.where(is_e, halo, pltpu.roll(flux_u, COLS - 1, 1))
        west = jnp.where(is_w, halo, pltpu.roll(flux_u, 1, 1))
        north = jnp.where(is_n, seam_rows[1, k : k + 1, :], pltpu.roll(flux_v, ROWS - 1, 0))
        south = jnp.where(is_s, seam_rows[4, k : k + 1, :], pltpu.roll(flux_v, 1, 0))
        new_th[k] = th[k] - half * ((east - west) + (north - south))
        for part, (begin, end) in enumerate(parts):
            if k == end - 1:
                rows = pl.ds(begin, end - begin)
                for n, (held, out) in enumerate(((new_u, new_u_hbm), (new_v, new_v_hbm), (new_th, new_th_hbm))):
                    copy = pltpu.make_async_copy(held.at[rows], out.at[rows], sems.at[n, part])
                    copy.start()
                    copies.append(copy)
    for copy in copies + plane_copies:
        copy.wait()


def vmem(count):
    return [pl.BlockSpec(memory_space=pltpu.VMEM)] * count


def hbm(count):
    return [pl.BlockSpec(memory_space=pltpu.HBM)] * count


def in_hbm(*arrays):
    return tuple(pltpu.with_memory_space_constraint(x, pltpu.HBM) for x in arrays)


def f32(*shape):
    return jax.ShapeDtypeStruct(shape, jnp.float32)


PARAMS = pltpu.CompilerParams(vmem_limit_bytes=40 * 2**20)


def local(lu, lv, th, lev, u, v, land, bottom, fold_map, gravity):
    lons, lats = lax.axis_size("lon"), lax.axis_size("lat")
    lon_msg, lat_msg = f32(LON_ROWS, COLS), f32(LAT_ROWS, COLS)
    layers, plane = f32(LAYERS, ROWS, COLS), f32(ROWS, COLS)
    held = pltpu.VMEM((LAYERS, ROWS, COLS), jnp.float32)
    total = lons * COLS
    pivot = fold_map[0] + lax.axis_index("lon") * COLS
    shift = jnp.mod(pivot - COLS // 2, total) // COLS

    msg_a, msg_b, own_pairs, own_rows, flat, cor, g_rows, tail_u, tail_v, weight, th, floor = pl.pallas_call(
        first_kernel,
        out_shape=(
            lon_msg, lon_msg, plane, f32(16, COLS), f32(8, ROWS, COLS), f32(FULL, COLS), f32(16, COLS),
            layers, layers, layers, layers,
            jax.ShapeDtypeStruct((2, ROWS, COLS), jnp.int32),
        ),
        in_specs=hbm(10),
        out_specs=vmem(12),
        scratch_shapes=[
            held,
            held,
            pltpu.SMEM((LAYERS,), jnp.float32),
            pltpu.SMEM((COLS,), jnp.int32),
            pltpu.SemaphoreType.DMA((10,)),
        ],
        compiler_params=PARAMS,
        name="edges",
    )(*in_hbm(gravity, lu, lv, th, lev, u, v, land, bottom, fold_map))

    got_a = lax.ppermute(msg_a, "lon", [(i, i ^ 1) for i in range(lons)])
    got_b = lax.ppermute(msg_b, "lon", [(i, (((i + 1) ^ 1) - 1) % lons) for i in range(lons)])
    got_a, got_b, shift = lax.optimization_barrier((got_a, got_b, shift))

    ext, edges, msg_x, msg_y, msg_f = pl.pallas_call(
        second_kernel,
        out_shape=(f32(6, ROWS, WIDE), f32(3, ROWS, COLS), lat_msg, lat_msg, lat_msg),
        in_specs=vmem(7),
        out_specs=vmem(5),
        compiler_params=PARAMS,
        name="extend",
    )(g_rows, flat, own_pairs, own_rows, msg_a, got_a, got_b)

    got_x = lax.ppermute(msg_x, "lat", [(i, i ^ 1) for i in range(lats)])
    top = lats - 1
    rows = [(b * lats + i, b * lats + ((i + 1) ^ 1) - 1) for b in range(lons) for i in range(1, top)]
    rows += [(b * lats, (b ^ 1) * lats) for b in range(lons)]

    def exchange(q):
        pairs = list(rows)
        for b in range(lons):
            source = (q - b) % lons
            source = (b + lons // 2) % lons if source == b else source
            pairs.append((source * lats + top, b * lats + top))
        return lambda x: lax.ppermute(x, ("lon", "lat"), pairs)

    got_f = lax.switch(shift, [exchange(q) for q in range(lons)], msg_f)

    padded = pltpu.VMEM((FULL + 16, WIDE), jnp.float32)
    rows16 = pltpu.VMEM((6, 16, COLS), jnp.float32)
    return pl.pallas_call(
        third_kernel,
        out_shape=(layers, layers, layers, plane, plane, plane),
        in_specs=vmem(14) + hbm(1),
        out_specs=hbm(6),
        scratch_shapes=[
            pltpu.VMEM((LAT_ROWS, COLS), jnp.float32),
            padded,
            padded,
            pltpu.VMEM((4, FULL, WIDE), jnp.float32),
            pltpu.VMEM((7, FULL, WIDE), jnp.float32),
            rows16,
            pltpu.VMEM((2, 16, WIDE), jnp.float32),
            rows16,
            held,
            held,
            held,
            pltpu.VMEM((3, ROWS, COLS), jnp.float32),
            pltpu.SemaphoreType.DMA((3, 4)),
            pltpu.SemaphoreType.DMA((3,)),
            pltpu.SemaphoreType.DMA((1,)),
        ],
        compiler_params=PARAMS,
        name="advance",
    )(g_rows, tail_u, tail_v, weight, th, floor, flat, cor, edges, ext, msg_x, msg_y, msg_f, got_x, *in_hbm(got_f))


def solution(mesh):
    layered, plane = P(None, "lat", "lon"), P("lat", "lon")
    return jax.shard_map(
        local,
        mesh=mesh,
        in_specs=(layered,) * 3 + (plane,) * 5 + (P("lon"), P()),
        out_specs=(layered,) * 3 + (plane,) * 3,
        check_vma=False,
    )
```

profile of v0, /device:TPU:6, one launch (start us, length us, event | category | flops | bytes accessed | tf_op | source)
XLA Modules:
  0.0 25.6 jit_solution(15242192564616137800)
XLA Ops:
  0.6 2.2 %edges.1 = (f32[152,128]{1,0:T(8,128)S(1)}, f32[152,128]{1,0:T(8,128)S(1)}, f32[64,128]{1,0:T(8,128)S(1)}, f32[16,128]{1,0:T(8,128)S(1)}, f32[8,64,128]{2,1,0:T(...) custom-call(f32[12]{0:T(128)} %gravity_hbm.1, ...), custom_call_target="tpu_custom_call" | custom-call | tf_op jit(solution)/shard_map/edges/pallas_call | solution.py:505
  2.8 8.0 %collective-permute-start.33 = (f32[152,128]{1,0:T(8,128)S(1)}, f32[152,128]{1,0:T(8,128)S(1)}, u32[]{:S(2)}, u32[]{:S(2)}) collective-permute-start(f32[152,128]{1,0:T(8,128)S(1)} %get-tuple-element.102), channel_id=1, source_target_pairs={{0,248},{8,16},{16,8},{24,32},{32,24},{40,48},{48,40},{56,64},{64,... | collective-permute-start | bytes 233480 | tf_op jit(solution)/shard_map/ppermute | solution.py:526
  10.8 0.0 collective-permute-start.32
  10.8 0.0 copy-start
  10.8 0.7 %copy-done = s32[128]{0:T(128)S(1)} copy-done((s32[128]{0:T(128)S(1)}, s32[128]{0:T(128)}, u32[]{:S(2)}) %copy-start) | copy-done | bytes 536
  11.6 1.3 %collective-permute-done.33.got_b = f32[152,128]{1,0:T(8,128)S(1)} collective-permute-done((f32[152,128]{1,0:T(8,128)S(1)}, f32[152,128]{1,0:T(8,128)S(1)}, u32[]{:S(2)}, u32[]{:S(2)}) %collective-permute-start.33) | collective-permute-done | bytes 77856 | tf_op jit(solution)/shard_map/ppermute | solution.py:526
  12.9 0.0 collective-permute-done.32.got_a
  12.9 0.9 %extend.1 = (f32[6,64,256]{2,1,0:T(8,128)S(1)}, f32[3,64,128]{2,1,0:T(8,128)S(1)}, f32[160,128]{1,0:T(8,128)S(1)}, f32[160,128]{1,0:T(8,128)S(1)}, f32[160,128]{1,0:T(8,128)S(1)}) custom-call(f32[16,128]{1,0:T(8,128)S(1)} %get-tuple-element.91.g_rows, f32[8,64,128]{2,1,0:T(8,128)S(1)} %get-tuple-element.97.flat, f32[64,128]{1,0:T(8,128)S(1)} %get-tuple-element.99.own_pairs, ...), custom_call_target="tpu_custom_call" | custom-call | tf_op jit(solution)/shard_map/extend/pallas_call | solution.py:529
  13.8 0.9 %collective-permute-start.34 = (f32[160,128]{1,0:T(8,128)S(1)}, f32[160,128]{1,0:T(8,128)S(1)}, u32[]{:S(2)}, u32[]{:S(2)}) collective-permute-start(f32[160,128]{1,0:T(8,128)S(1)} %get-tuple-element.107.own_x), channel_id=1, source_target_pairs={{0,1},{1,0},{2,3},{3,2},{4,5},{5,4},{6,7},{7,6},{8,9},{9,8},{10,11... | collective-permute-start | bytes 245768 | tf_op jit(solution)/shard_map/ppermute | solution.py:538
  14.7 6.7 %conditional.1 = (f32[160,128]{1,0:T(8,128)}) conditional(s32[]{:T(128)} %clamp.3, f32[160,128]{1,0:T(8,128)S(1)} %get-tuple-element.109.own_f, f32[160,128]{1,0:T(8,128)S(1)} %get-tuple-element.109.own_f, f32[160,128]{1,0:T(8,128)S(1)} %get-tuple-element.109.own_f, ...), branch_computations={%region_0.1_spmd, %region_1.2_spmd, %region_2.3_spmd, %region_3.4_... | conditional | bytes 327728 | solution.py:551
  14.7 1.3 %collective-permute-start.10 = (f32[160,128]{1,0:T(8,128)S(1)}, f32[160,128]{1,0:T(8,128)}, u32[]{:S(2)}, u32[]{:S(2)}) collective-permute-start(f32[160,128]{1,0:T(8,128)S(1)} %param.10), channel_id=1, source_target_pairs={{1,2},{2,1},{3,4},{4,3},{5,6},{6,5},{9,10},{10,9},{11,12},{12,11},... | collective-permute-start | bytes 245768 | tf_op jit(solution)/shard_map/cond/branch_10_fun/ppermute | solution.py:549
  16.0 5.4 %collective-permute-done.10 = f32[160,128]{1,0:T(8,128)} collective-permute-done((f32[160,128]{1,0:T(8,128)S(1)}, f32[160,128]{1,0:T(8,128)}, u32[]{:S(2)}, u32[]{:S(2)}) %collective-permute-start.10) | collective-permute-done | bytes 81952 | tf_op jit(solution)/shard_map/cond/branch_10_fun/ppermute | solution.py:549
  21.4 0.0 collective-permute-done.34.got_x
  21.4 4.1 %advance.1 = (f32[12,64,128]{2,1,0:T(8,128)}, f32[12,64,128]{2,1,0:T(8,128)}, f32[12,64,128]{2,1,0:T(8,128)}, f32[64,128]{1,0:T(8,128)}, f32[64,128]{1,0:T(8,128)}, /*index=5*/f32[64,128]{1,0:T(8,128)}) custom-call(f32[16,128]{1,0:T(8,128)S(1)} %get-tuple-element.91.g_rows, f32[12,64,128]{2,1,0:T(8,128)S(1)} %get-tuple-element.92.tail_u, ...), custom_call_target="tpu_custom_call" | custom-call | tf_op jit(solution)/shard_map/advance/pallas_call | solution.py:555
Async XLA Ops:
  2.8 10.1 %collective-permute-start.33 = (f32[152,128]{1,0:T(8,128)S(1)}, f32[152,128]{1,0:T(8,128)S(1)}, u32[]{:S(2)}, u32[]{:S(2)}) collective-permute-start(f32[152,128]{1,0:T(8,128)S(1)} %get-tuple-element.102), channel_id=1, source_target_pairs={{0,248},{8,16},{16,8},{24,32},{32,24},{40,48},{48,40},{56,64},{64,... | collective-permute-start | bytes 233480 | tf_op jit(solution)/shard_map/ppermute | solution.py:526
  10.8 2.1 %collective-permute-start.32 = (f32[152,128]{1,0:T(8,128)S(1)}, f32[152,128]{1,0:T(8,128)S(1)}, u32[]{:S(2)}, u32[]{:S(2)}) collective-permute-start(f32[152,128]{1,0:T(8,128)S(1)} %get-tuple-element.101.own_a), channel_id=1, source_target_pairs={{0,8},{8,0},{16,24},{24,16},{32,40},{40,32},{48,56},{56,48},{64,72... | collective-permute-start | bytes 233480 | tf_op jit(solution)/shard_map/ppermute | solution.py:525
  10.8 0.7 %copy-start = (s32[128]{0:T(128)S(1)}, s32[128]{0:T(128)}, u32[]{:S(2)}) copy-start(s32[128]{0:T(128)} %fold_hbm.1) | copy-start | bytes 1540
  13.8 7.6 %collective-permute-start.34 = (f32[160,128]{1,0:T(8,128)S(1)}, f32[160,128]{1,0:T(8,128)S(1)}, u32[]{:S(2)}, u32[]{:S(2)}) collective-permute-start(f32[160,128]{1,0:T(8,128)S(1)} %get-tuple-element.107.own_x), channel_id=1, source_target_pairs={{0,1},{1,0},{2,3},{3,2},{4,5},{5,4},{6,7},{7,6},{8,9},{9,8},{10,11... | collective-permute-start | bytes 245768 | tf_op jit(solution)/shard_map/ppermute | solution.py:538
  14.7 6.7 %collective-permute-start.10 = (f32[160,128]{1,0:T(8,128)S(1)}, f32[160,128]{1,0:T(8,128)}, u32[]{:S(2)}, u32[]{:S(2)}) collective-permute-start(f32[160,128]{1,0:T(8,128)S(1)} %param.10), channel_id=1, source_target_pairs={{1,2},{2,1},{3,4},{4,3},{5,6},{6,5},{9,10},{10,9},{11,12},{12,11},... | collective-permute-start | bytes 245768 | tf_op jit(solution)/shard_map/cond/branch_10_fun/ppermute | solution.py:549
where the time goes:
time: 25.8 us; the launch traced here: 25.6 us
  starting transfers between devices  10.2 us (40%)
  Pallas kernels  7.13 us (28%)
  waiting for transfers between devices  6.75 us (26%)
  between operations  0.89 us (3%)
  local copies, waits for them, and re-layouts  0.66 us (3%)
    ppermute x1, starting transfers between devices, local(): lax.ppermute(msg_b, 'lon', [(i, ((i + 1 ^ 1) - 1) % lons) for i in range(...  8.01 us
    ppermute x1, waiting for transfers between devices, exchange(): return lambda x: lax.ppermute(x, ('lon', 'lat'), pairs)  5.4 us
    pallas_call x1, Pallas kernels, local(): pl.pallas_call(third_kernel, out_shape=(layers, layers, layers, plane, pl...  4.1 us
    pallas_call x1, Pallas kernels, local(): pl.pallas_call(first_kernel, out_shape=(lon_msg, lon_msg, plane, f32(16,...  2.18 us
    ppermute x1, waiting for transfers between devices, local(): lax.ppermute(msg_b, 'lon', [(i, ((i + 1 ^ 1) - 1) % lons) for i in range(...  1.35 us
    ppermute x1, starting transfers between devices, exchange(): return lambda x: lax.ppermute(x, ('lon', 'lat'), pairs)  1.25 us
    ppermute x1, starting transfers between devices, local(): got_x = lax.ppermute(msg_x, 'lat', [(i, i ^ 1) for i in range(lats)])  0.92 us
    pallas_call x1, Pallas kernels, local(): pl.pallas_call(second_kernel, out_shape=(f32(6, ROWS, WIDE), f32(3, ROWS,...  0.86 us
  transfers between devices with their start and end apart: 4, of which 2 were waited for; matrix products, arithmetic and copies ran while one was open for 0% of the time, Pallas kernels for 0%

commit v1 on v0

--- a/solution.py
+++ b/solution.py
@@ -24,6 +24,7 @@
 FULL = ROWS + 2 * HALO
 WIDE = 2 * COLS
 half = 0.5 * baroclinic_step
+FAR_PARTS = 5
 
 
 def lane_index(shape):
@@ -41,7 +42,7 @@
 
 def first_kernel(
     gravity_hbm, lu_hbm, lv_hbm, th_hbm, lev_hbm, u_hbm, v_hbm, land_hbm, bottom_hbm, fold_hbm,
-    msg_a, msg_b, own_pairs, own_rows, flat, cor_out, g_rows, tail_u, tail_v, weight, th, floor,
+    msg_a, msg_b, own_pairs, own_rows, flat, cor_out, g_rows, to_potential, tail_u, tail_v, weight, th, floor,
     lu, lv, gravity, fold, sems,
 ):
     pairs = (
@@ -60,18 +61,25 @@
     cor = cor_all[HALO : HALO + ROWS]
     lane = lane_index((ROWS, COLS))
     row = row_index((ROWS, COLS))
-    for copy in copies:
+    copies[3].wait()
+    line = (lane_index((COLS, COLS)) - PAIR_LANE) >> 1
+    at = (row_index((COLS, COLS)) - PAIR_LANE) >> 1
+    upper, lower = jnp.zeros((COLS, COLS), jnp.float32), jnp.zeros((COLS, COLS), jnp.float32)
+    total = 0.0
+    for k in range(LAYERS):
+        g_rows[k : k + 1, :] = jnp.full((1, COLS), gravity[k], jnp.float32)
+        lower = jnp.where(at == k, total, lower)
+        total = total + gravity[k]
+        upper = jnp.where(line == k, total, upper)
+    used = (at >= 0) & (at <= line) & (line < LAYERS) & (((lane_index((COLS, COLS)) - row_index((COLS, COLS))) & 1) == 0)
+    to_potential[...] = jnp.where(used, upper - lower, 0.0)
+    for copy in copies[:3] + copies[4:]:
         copy.wait()
     wet = floor[0].astype(jnp.float32)
     bot = floor[1]
     lev, u, v = flat[5], flat[6], flat[7]
     zero = jnp.zeros((ROWS, COLS), jnp.float32)
-    line = lane_index((1, COLS))
-    lanes_g = jnp.zeros((1, COLS), jnp.float32)
-    for k in range(LAYERS):
-        g_rows[k : k + 1, :] = jnp.full((1, COLS), gravity[k], jnp.float32)
-        lanes_g = jnp.where((line - PAIR_LANE) >> 1 == k, gravity[k], lanes_g)
-    g_rows[LAYERS : LAYERS + 1, :] = lanes_g
+    g_rows[LAYERS : LAYERS + 1, :] = jnp.zeros((1, COLS), jnp.float32)
     offset = 64 + ((fold[0] + 64) & (COLS - 1))
     g_rows[LAYERS + 1 : LAYERS + 2, :] = jnp.full((1, COLS), offset, jnp.int32).astype(jnp.float32)
     lons = lax.axis_size("lon")
@@ -161,13 +169,7 @@
     own_rows[V_BOTTOM + 1 :] = jnp.zeros((16 - V_BOTTOM - 1, COLS), jnp.float32)
 
 
-def lane_prefix(x):
-    for shift in (2, 4, 8, 16):
-        x = x + pltpu.roll(x, shift, 1)
-    return x
-
-
-def second_kernel(g_rows, flat, own_pairs, own_rows, own_a, got_a, got_b, ext, edges, msg_x, msg_y, msg_f):
+def second_kernel(g_rows, to_potential, flat, own_pairs, own_rows, own_a, got_a, got_b, ext, edges, msg_x, msg_y, msg_f):
     lon, lat = lax.axis_index("lon"), lax.axis_index("lat")
     even_lon = lax.rem(lon, 2) == 0
     even_lat = lax.rem(lat, 2) == 0
@@ -175,12 +177,8 @@
     is_pair = (lane >= PAIR_LANE) & (lane < PAIR_END)
     is_odd = lane % 2 == 1
     sign = jnp.where(is_odd, -1.0, 1.0)
-    weights_g = g_rows[LAYERS : LAYERS + 1, :]
     east = jnp.where(even_lon, got_a[:ROWS], got_b[:ROWS])
     west = jnp.where(even_lon, got_b[:ROWS], got_a[:ROWS])
-
-    def potentials(w):
-        return lane_prefix(weights_g * lane_prefix(w))
 
     def dots(x):
         even_sum = jnp.sum(jnp.where(is_odd, 0.0, x), axis=1, keepdims=True)
@@ -191,7 +189,9 @@
     w_halo = jnp.where(is_pair, jnp.where(is_odd, roll(west, apart + 1, 1), east), 0.0)
     c_halo = jnp.where(is_odd, roll(west, apart, 1), roll(east, -1, 1))
     w_own = roll(own_pairs[...], PAIR_LANE, 1)
-    p_halo, p_own = potentials(w_halo), potentials(w_own)
+    both = jnp.concatenate([w_halo, w_own], axis=0)
+    both = jnp.dot(both, to_potential[...], precision=lax.Precision.HIGHEST, preferred_element_type=jnp.float32)
+    p_halo, p_own = both[:ROWS], both[ROWS:]
     edges[0] = (-half * sign) * p_halo
     edges[1] = w_halo * (c_halo + (half * sign) * p_own)
     edges[2] = w_halo
@@ -247,23 +247,24 @@
         lat_message(msg_x, False)
         lat_message(msg_y, True)
 
+
     @pl.when(lat == lax.axis_size("lat") - 1)
     def _():
         lane8 = lane_index((8, COLS))
         row8 = row_index((8, COLS))
         offset = jnp.broadcast_to(g_rows[LAYERS + 1 : LAYERS + 2, :].astype(jnp.int32), (8, COLS))
         source = (offset - lane8) & (COLS - 1)
-        block = (COLS + offset - lane8) >> 7
-        side_block = jnp.where(lane8 < HALO, offset - lane8, 2 * COLS + offset - lane8) >> 7
+        taker = source
+        block = (COLS + offset - taker) >> 7
+        side_block = jnp.where(taker < HALO, offset - taker, 2 * COLS + offset - taker) >> 7
 
         def gather(x, index, axis):
             return jnp.take_along_axis(x, index, axis=axis, mode="promise_in_bounds")
 
         def window(w_tile, o_tile, e_tile):
-            a, b, c = gather(w_tile, source, 1), gather(o_tile, source, 1), gather(e_tile, source, 1)
-            main = jnp.where(block == 0, a, jnp.where(block == 1, b, c))
-            side = jnp.where(side_block == 0, a, jnp.where(side_block == 1, b, c))
-            return main, side
+            main = jnp.where(block == 0, w_tile, jnp.where(block == 1, o_tile, e_tile))
+            side = jnp.where(side_block == 0, w_tile, jnp.where(side_block == 1, o_tile, e_tile))
+            return gather(main, source, 1), gather(side, source, 1)
 
         def tiles(at):
             on_e = jnp.where(even_lon, got_a[at : at + 8, :], got_b[at : at + 8, :])
@@ -315,8 +316,12 @@
     at_top = lat == lax.axis_size("lat") - 1
     at_bottom = lat == 0
 
-    fold_copy = pltpu.make_async_copy(got_f_hbm, far, far_sem.at[0])
-    fold_copy.start()
+    far_copies = []
+    for n in range(FAR_PARTS):
+        part = pl.ds(n * (LAT_ROWS // FAR_PARTS), LAT_ROWS // FAR_PARTS)
+        far_copies.append(pltpu.make_async_copy(got_f_hbm.at[part], far.at[part], far_sem.at[n]))
+    for copy in far_copies:
+        copy.start()
     inner = slice(HALO, HALO + ROWS)
 
     def place(at, count, depth, u, v, level, force_u, force_v, rate):
@@ -389,28 +394,32 @@
         seam_rows[side + 2, :LAYERS, :] = w
 
     strip(got_x, own_x, 0, even, None)
-    fold_copy.wait()
+    for copy in far_copies:
+        copy.wait()
 
     far[...] = jnp.where(at_top & (g_rows[LAYERS + 2 : LAYERS + 3, :] > 0.0), own_f[...], far[...])
     strip(far, own_y, 1, jnp.logical_not(even), jnp.logical_not(at_bottom))
 
     for step in range(SUBSTEPS):
-        depth, u, v = fixed[0], state[0], state[1]
+        skip = (2 * step) // 8 * 8
+        count = FULL - 2 * skip
+        rows = slice(skip, skip + count)
+        depth, u, v = fixed[0, rows, :], state[0, rows, :], state[1, rows, :]
         trans_u = depth * u
-        v_pad[8 : 8 + FULL, :] = depth * v
-        dv = v_pad[9 : 9 + FULL, :] - v_pad[7 : 7 + FULL, :]
+        v_pad[8 + skip : 8 + skip + count, :] = depth * v
+        dv = v_pad[9 + skip : 9 + skip + count, :] - v_pad[7 + skip : 7 + skip + count, :]
         du = pltpu.roll(trans_u, WIDE - 1, 1) - pltpu.roll(trans_u, 1, 1)
-        level = level_pad[8 : 8 + FULL, :] - fixed[6] * (du + dv)
-        level_pad[8 : 8 + FULL, :] = level
-        dy = level_pad[9 : 9 + FULL, :] - level_pad[7 : 7 + FULL, :]
+        level = level_pad[8 + skip : 8 + skip + count, :] - fixed[6, rows, :] * (du + dv)
+        level_pad[8 + skip : 8 + skip + count, :] = level
+        dy = level_pad[9 + skip : 9 + skip + count, :] - level_pad[7 + skip : 7 + skip + count, :]
         dx = pltpu.roll(level, WIDE - 1, 1) - pltpu.roll(level, 1, 1)
-        keep, turn, slope = fixed[1], fixed[2], fixed[5]
-        next_u = keep * u + turn * v + fixed[3] - slope * dx
-        next_v = keep * v - turn * u + fixed[4] - slope * dy
-        state[0] = next_u
-        state[1] = next_v
-        state[2] = next_u if step == 0 else state[2] + next_u
-        state[3] = next_v if step == 0 else state[3] + next_v
+        keep, turn, slope = fixed[1, rows, :], fixed[2, rows, :], fixed[5, rows, :]
+        next_u = keep * u + turn * v + fixed[3, rows, :] - slope * dx
+        next_v = keep * v - turn * u + fixed[4, rows, :] - slope * dy
+        state[0, rows, :] = next_u
+        state[1, rows, :] = next_v
+        state[2, rows, :] = next_u if step == 0 else state[2, rows, :] + next_u
+        state[3, rows, :] = next_v if step == 0 else state[3, rows, :] + next_v
     planes[0] = level_pad[8 + HALO : 8 + HALO + ROWS, :COLS]
     planes[1] = state[2, inner, :COLS] * (1.0 / SUBSTEPS)
     planes[2] = state[3, inner, :COLS] * (1.0 / SUBSTEPS)
@@ -502,15 +511,15 @@
     pivot = fold_map[0] + lax.axis_index("lon") * COLS
     shift = jnp.mod(pivot - COLS // 2, total) // COLS
 
-    msg_a, msg_b, own_pairs, own_rows, flat, cor, g_rows, tail_u, tail_v, weight, th, floor = pl.pallas_call(
+    msg_a, msg_b, own_pairs, own_rows, flat, cor, g_rows, to_potential, tail_u, tail_v, weight, th, floor = pl.pallas_call(
         first_kernel,
         out_shape=(
-            lon_msg, lon_msg, plane, f32(16, COLS), f32(8, ROWS, COLS), f32(FULL, COLS), f32(16, COLS),
+            lon_msg, lon_msg, plane, f32(16, COLS), f32(8, ROWS, COLS), f32(FULL, COLS), f32(16, COLS), f32(COLS, COLS),
             layers, layers, layers, layers,
             jax.ShapeDtypeStruct((2, ROWS, COLS), jnp.int32),
         ),
         in_specs=hbm(10),
-        out_specs=vmem(12),
+        out_specs=vmem(13),
         scratch_shapes=[
             held,
             held,
@@ -529,11 +538,11 @@
     ext, edges, msg_x, msg_y, msg_f = pl.pallas_call(
         second_kernel,
         out_shape=(f32(6, ROWS, WIDE), f32(3, ROWS, COLS), lat_msg, lat_msg, lat_msg),
-        in_specs=vmem(7),
+        in_specs=vmem(8),
         out_specs=vmem(5),
         compiler_params=PARAMS,
         name="extend",
-    )(g_rows, flat, own_pairs, own_rows, msg_a, got_a, got_b)
+    )(g_rows, to_potential, flat, own_pairs, own_rows, msg_a, got_a, got_b)
 
     got_x = lax.ppermute(msg_x, "lat", [(i, i ^ 1) for i in range(lats)])
     top = lats - 1
@@ -572,7 +581,7 @@
             pltpu.VMEM((3, ROWS, COLS), jnp.float32),
             pltpu.SemaphoreType.DMA((3, 4)),
             pltpu.SemaphoreType.DMA((3,)),
-            pltpu.SemaphoreType.DMA((1,)),
+            pltpu.SemaphoreType.DMA((FAR_PARTS,)),
         ],
         compiler_params=PARAMS,
         name="advance",

time: 25.8 us -> 25.4 us (0.984)
  Pallas kernels: 7.13 us -> 6.74 us
    pallas_call x1, Pallas kernels: 0.86 us -> 0.49 us  [local(): pl.pallas_call(second_kernel, out_shape=(f32(6, ROWS, WIDE), f32(3, ROWS,...]
where the time goes in v1:
time: 25.4 us; the launch traced here: 25.2 us
  starting transfers between devices  10.2 us (40%)
  waiting for transfers between devices  6.76 us (27%)
  Pallas kernels  6.74 us (27%)
  between operations  0.89 us (4%)
  local copies, waits for them, and re-layouts  0.66 us (3%)
    ppermute x1, starting transfers between devices, local(): lax.ppermute(msg_b, 'lon', [(i, ((i + 1 ^ 1) - 1) % lons) for i in range(...  8.01 us
    ppermute x1, waiting for transfers between devices, exchange(): return lambda x: lax.ppermute(x, ('lon', 'lat'), pairs)  5.41 us
    pallas_call x1, Pallas kernels, local(): pl.pallas_call(third_kernel, out_shape=(layers, layers, layers, plane, pl...  4.07 us
    pallas_call x1, Pallas kernels, local(): pl.pallas_call(first_kernel, out_shape=(lon_msg, lon_msg, plane, f32(16,...  2.18 us
    ppermute x1, waiting for transfers between devices, local(): lax.ppermute(msg_b, 'lon', [(i, ((i + 1 ^ 1) - 1) % lons) for i in range(...  1.35 us
    ppermute x1, starting transfers between devices, exchange(): return lambda x: lax.ppermute(x, ('lon', 'lat'), pairs)  1.25 us
    ppermute x1, starting transfers between devices, local(): got_x = lax.ppermute(msg_x, 'lat', [(i, i ^ 1) for i in range(lats)])  0.92 us
    unnamed x2, local copies, waits for them, and re-layouts  0.66 us
  transfers between devices with their start and end apart: 4, of which 2 were waited for; matrix products, arithmetic and copies ran while one was open for 0% of the time, Pallas kernels for 0%

profile of v1, /device:TPU:6, one launch (start us, length us, event | category | flops | bytes accessed | tf_op | source)
XLA Modules:
  0.0 25.2 jit_solution(199281067005254163)
XLA Ops:
  0.6 2.2 %edges.1 = (f32[152,128]{1,0:T(8,128)S(1)}, f32[152,128]{1,0:T(8,128)S(1)}, f32[64,128]{1,0:T(8,128)S(1)}, f32[16,128]{1,0:T(8,128)S(1)}, f32[8,64,128]{2,1,0:T(...) custom-call(f32[12]{0:T(128)} %gravity_hbm.1, ...), custom_call_target="tpu_custom_call" | custom-call | tf_op jit(solution)/shard_map/edges/pallas_call | solution.py:514
  2.8 8.0 %collective-permute-start.33 = (f32[152,128]{1,0:T(8,128)S(1)}, f32[152,128]{1,0:T(8,128)S(1)}, u32[]{:S(2)}, u32[]{:S(2)}) collective-permute-start(f32[152,128]{1,0:T(8,128)S(1)} %get-tuple-element.104), channel_id=1, source_target_pairs={{0,248},{8,16},{16,8},{24,32},{32,24},{40,48},{48,40},{56,64},{64,... | collective-permute-start | bytes 233480 | tf_op jit(solution)/shard_map/ppermute | solution.py:535
  10.8 0.0 collective-permute-start.32
  10.8 0.0 copy-start
  10.8 0.7 %copy-done = s32[128]{0:T(128)S(1)} copy-done((s32[128]{0:T(128)S(1)}, s32[128]{0:T(128)}, u32[]{:S(2)}) %copy-start) | copy-done | bytes 536
  11.6 1.3 %collective-permute-done.33.got_b = f32[152,128]{1,0:T(8,128)S(1)} collective-permute-done((f32[152,128]{1,0:T(8,128)S(1)}, f32[152,128]{1,0:T(8,128)S(1)}, u32[]{:S(2)}, u32[]{:S(2)}) %collective-permute-start.33) | collective-permute-done | bytes 77856 | tf_op jit(solution)/shard_map/ppermute | solution.py:535
  12.9 0.0 collective-permute-done.32.got_a
  12.9 0.5 %extend.1 = (f32[6,64,256]{2,1,0:T(8,128)S(1)}, f32[3,64,128]{2,1,0:T(8,128)S(1)}, f32[160,128]{1,0:T(8,128)S(1)}, f32[160,128]{1,0:T(8,128)S(1)}, f32[160,128]{1,0:T(8,128)S(1)}) custom-call(f32[16,128]{1,0:T(8,128)S(1)} %get-tuple-element.92.g_rows, f32[128,128]{1,0:T(8,128)S(1)} %get-tuple-element.100.to_potential, ...), custom_call_target="tpu_custom_call" | custom-call | tf_op jit(solution)/shard_map/extend/pallas_call | solution.py:538
  13.4 0.9 %collective-permute-start.34 = (f32[160,128]{1,0:T(8,128)S(1)}, f32[160,128]{1,0:T(8,128)S(1)}, u32[]{:S(2)}, u32[]{:S(2)}) collective-permute-start(f32[160,128]{1,0:T(8,128)S(1)} %get-tuple-element.109.own_x), channel_id=1, source_target_pairs={{0,1},{1,0},{2,3},{3,2},{4,5},{5,4},{6,7},{7,6},{8,9},{9,8},{10,11... | collective-permute-start | bytes 245768 | tf_op jit(solution)/shard_map/ppermute | solution.py:547
  14.3 6.7 %conditional.1 = (f32[160,128]{1,0:T(8,128)}) conditional(s32[]{:T(128)} %clamp.3, f32[160,128]{1,0:T(8,128)S(1)} %get-tuple-element.111.own_f, f32[160,128]{1,0:T(8,128)S(1)} %get-tuple-element.111.own_f, f32[160,128]{1,0:T(8,128)S(1)} %get-tuple-element.111.own_f, ...), branch_computations={%region_0.1_spmd, %region_1.2_spmd, %region_2.3_spmd, %region_3.4_... | conditional | bytes 327728 | solution.py:560
  14.3 1.2 %collective-permute-start.14 = (f32[160,128]{1,0:T(8,128)S(1)}, f32[160,128]{1,0:T(8,128)}, u32[]{:S(2)}, u32[]{:S(2)}) collective-permute-start(f32[160,128]{1,0:T(8,128)S(1)} %param.14), channel_id=1, source_target_pairs={{1,2},{2,1},{3,4},{4,3},{5,6},{6,5},{9,10},{10,9},{11,12},{12,11},... | collective-permute-start | bytes 245768 | tf_op jit(solution)/shard_map/cond/branch_14_fun/ppermute | solution.py:558
  15.6 5.4 %collective-permute-done.14 = f32[160,128]{1,0:T(8,128)} collective-permute-done((f32[160,128]{1,0:T(8,128)S(1)}, f32[160,128]{1,0:T(8,128)}, u32[]{:S(2)}, u32[]{:S(2)}) %collective-permute-start.14) | collective-permute-done | bytes 81952 | tf_op jit(solution)/shard_map/cond/branch_14_fun/ppermute | solution.py:558
  21.0 0.0 collective-permute-done.34.got_x
  21.0 4.1 %advance.1 = (f32[12,64,128]{2,1,0:T(8,128)}, f32[12,64,128]{2,1,0:T(8,128)}, f32[12,64,128]{2,1,0:T(8,128)}, f32[64,128]{1,0:T(8,128)}, f32[64,128]{1,0:T(8,128)}, /*index=5*/f32[64,128]{1,0:T(8,128)}) custom-call(f32[16,128]{1,0:T(8,128)S(1)} %get-tuple-element.92.g_rows, f32[12,64,128]{2,1,0:T(8,128)S(1)} %get-tuple-element.93.tail_u, ...), custom_call_target="tpu_custom_call" | custom-call | tf_op jit(solution)/shard_map/advance/pallas_call | solution.py:564
Async XLA Ops:
  2.8 10.1 %collective-permute-start.33 = (f32[152,128]{1,0:T(8,128)S(1)}, f32[152,128]{1,0:T(8,128)S(1)}, u32[]{:S(2)}, u32[]{:S(2)}) collective-permute-start(f32[152,128]{1,0:T(8,128)S(1)} %get-tuple-element.104), channel_id=1, source_target_pairs={{0,248},{8,16},{16,8},{24,32},{32,24},{40,48},{48,40},{56,64},{64,... | collective-permute-start | bytes 233480 | tf_op jit(solution)/shard_map/ppermute | solution.py:535
  10.8 2.1 %collective-permute-start.32 = (f32[152,128]{1,0:T(8,128)S(1)}, f32[152,128]{1,0:T(8,128)S(1)}, u32[]{:S(2)}, u32[]{:S(2)}) collective-permute-start(f32[152,128]{1,0:T(8,128)S(1)} %get-tuple-element.103.own_a), channel_id=1, source_target_pairs={{0,8},{8,0},{16,24},{24,16},{32,40},{40,32},{48,56},{56,48},{64,72... | collective-permute-start | bytes 233480 | tf_op jit(solution)/shard_map/ppermute | solution.py:534
  10.8 0.7 %copy-start = (s32[128]{0:T(128)S(1)}, s32[128]{0:T(128)}, u32[]{:S(2)}) copy-start(s32[128]{0:T(128)} %fold_hbm.1) | copy-start | bytes 1540
  13.4 7.6 %collective-permute-start.34 = (f32[160,128]{1,0:T(8,128)S(1)}, f32[160,128]{1,0:T(8,128)S(1)}, u32[]{:S(2)}, u32[]{:S(2)}) collective-permute-start(f32[160,128]{1,0:T(8,128)S(1)} %get-tuple-element.109.own_x), channel_id=1, source_target_pairs={{0,1},{1,0},{2,3},{3,2},{4,5},{5,4},{6,7},{7,6},{8,9},{9,8},{10,11... | collective-permute-start | bytes 245768 | tf_op jit(solution)/shard_map/ppermute | solution.py:547
  14.3 6.7 %collective-permute-start.14 = (f32[160,128]{1,0:T(8,128)S(1)}, f32[160,128]{1,0:T(8,128)}, u32[]{:S(2)}, u32[]{:S(2)}) collective-permute-start(f32[160,128]{1,0:T(8,128)S(1)} %param.14), channel_id=1, source_target_pairs={{1,2},{2,1},{3,4},{4,3},{5,6},{6,5},{9,10},{10,9},{11,12},{12,11},... | collective-permute-start | bytes 245768 | tf_op jit(solution)/shard_map/cond/branch_14_fun/ppermute | solution.py:558

commit v2 on v1

--- a/solution.py
+++ b/solution.py
@@ -308,7 +308,7 @@
 def third_kernel(
     g_rows, tail_u, tail_v, weight, th, floor, flat, cor_ref, edges, ext, own_x, own_y, own_f, got_x, got_f_hbm,
     new_u_hbm, new_v_hbm, new_th_hbm, new_lev_hbm, mean_u_hbm, mean_v_hbm,
-    far, level_pad, v_pad, state, fixed, pots, seam_w, seam_rows, new_u, new_v, new_th, planes,
+    far, level_pad, v_pad, state, fixed, pots, seam_w, seam_rows, new_u, new_v, new_th, flux_v_pad, planes,
     sems, plane_sems, far_sem,
 ):
     lat = lax.axis_index("lat")
@@ -400,26 +400,33 @@
     far[...] = jnp.where(at_top & (g_rows[LAYERS + 2 : LAYERS + 3, :] > 0.0), own_f[...], far[...])
     strip(far, own_y, 1, jnp.logical_not(even), jnp.logical_not(at_bottom))
 
+    def blocks(skip):
+        edges_at = list(range(skip, FULL - skip, 8)) + [FULL - skip]
+        return list(zip(edges_at[:-1], edges_at[1:]))
+
+    for begin, end in blocks(0):
+        v_pad[8 + begin : 8 + end, :] = fixed[0, begin:end, :] * state[1, begin:end, :]
     for step in range(SUBSTEPS):
         skip = (2 * step) // 8 * 8
-        count = FULL - 2 * skip
-        rows = slice(skip, skip + count)
-        depth, u, v = fixed[0, rows, :], state[0, rows, :], state[1, rows, :]
-        trans_u = depth * u
-        v_pad[8 + skip : 8 + skip + count, :] = depth * v
-        dv = v_pad[9 + skip : 9 + skip + count, :] - v_pad[7 + skip : 7 + skip + count, :]
-        du = pltpu.roll(trans_u, WIDE - 1, 1) - pltpu.roll(trans_u, 1, 1)
-        level = level_pad[8 + skip : 8 + skip + count, :] - fixed[6, rows, :] * (du + dv)
-        level_pad[8 + skip : 8 + skip + count, :] = level
-        dy = level_pad[9 + skip : 9 + skip + count, :] - level_pad[7 + skip : 7 + skip + count, :]
-        dx = pltpu.roll(level, WIDE - 1, 1) - pltpu.roll(level, 1, 1)
-        keep, turn, slope = fixed[1, rows, :], fixed[2, rows, :], fixed[5, rows, :]
-        next_u = keep * u + turn * v + fixed[3, rows, :] - slope * dx
-        next_v = keep * v - turn * u + fixed[4, rows, :] - slope * dy
-        state[0, rows, :] = next_u
-        state[1, rows, :] = next_v
-        state[2, rows, :] = next_u if step == 0 else state[2, rows, :] + next_u
-        state[3, rows, :] = next_v if step == 0 else state[3, rows, :] + next_v
+        for begin, end in blocks(skip):
+            trans_u = fixed[0, begin:end, :] * state[0, begin:end, :]
+            dv = v_pad[9 + begin : 9 + end, :] - v_pad[7 + begin : 7 + end, :]
+            du = pltpu.roll(trans_u, WIDE - 1, 1) - pltpu.roll(trans_u, 1, 1)
+            held = level_pad[8 + begin : 8 + end, :]
+            level_pad[8 + begin : 8 + end, :] = held - fixed[6, begin:end, :] * (du + dv)
+        for begin, end in blocks(skip):
+            u, v = state[0, begin:end, :], state[1, begin:end, :]
+            level = level_pad[8 + begin : 8 + end, :]
+            dy = level_pad[9 + begin : 9 + end, :] - level_pad[7 + begin : 7 + end, :]
+            dx = pltpu.roll(level, WIDE - 1, 1) - pltpu.roll(level, 1, 1)
+            keep, turn, slope = fixed[1, begin:end, :], fixed[2, begin:end, :], fixed[5, begin:end, :]
+            next_u = keep * u + turn * v + fixed[3, begin:end, :] - slope * dx
+            next_v = keep * v - turn * u + fixed[4, begin:end, :] - slope * dy
+            state[0, begin:end, :] = next_u
+            state[1, begin:end, :] = next_v
+            state[2, begin:end, :] = next_u if step == 0 else state[2, begin:end, :] + next_u
+            state[3, begin:end, :] = next_v if step == 0 else state[3, begin:end, :] + next_v
+            v_pad[8 + begin : 8 + end, :] = fixed[0, begin:end, :] * next_v
     planes[0] = level_pad[8 + HALO : 8 + HALO + ROWS, :COLS]
     planes[1] = state[2, inner, :COLS] * (1.0 / SUBSTEPS)
     planes[2] = state[3, inner, :COLS] * (1.0 / SUBSTEPS)
@@ -439,8 +446,6 @@
     lane = lane_index((ROWS, COLS))
     row = row_index((ROWS, COLS))
     is_e, is_w = lane == COLS - 1, lane == 0
-    is_n, is_s = row == ROWS - 1, row == 0
-    is_edge = is_e | is_w
     base_u = rest(0, inner, main) - flat[3]
     base_v = rest(1, inner, main) - flat[4]
     side_u = rest(0, inner, beside)
@@ -455,23 +460,37 @@
     levels = jnp.where(floor[0] > 0, floor[1], 0)
     copies = []
     parts = ((0, 4), (4, 8), (8, 11), (11, 12))
+    lanes16 = lane_index((32, COLS))
+    rows16 = row_index((32, COLS))
+    is_e, is_w = lanes16 == COLS - 1, lanes16 == 0
+    is_edge = is_e | is_w
     for k in range(LAYERS):
-        w = weight[k]
-        mask = levels > k
         shift = COLS - 1 - PAIR_LANE - 2 * k
-        fix_u = jnp.where(is_edge, roll(pair_fix, shift, 1), 0.0)
-        fix_v = jnp.where(is_n, seam_rows[0, k : k + 1, :], jnp.where(is_s, seam_rows[3, k : k + 1, :], 0.0))
-        out_u = jnp.where(mask, tail_u[k] + base_u + fix_u, 0.0)
-        out_v = jnp.where(mask, tail_v[k] + base_v + fix_v, 0.0)
-        new_u[k] = out_u
-        new_v[k] = out_v
-        flux_u, flux_v = w * out_u, w * out_v
-        halo = roll(pair_flux, shift, 1)
-        east = jnp.where(is_e, halo, pltpu.roll(flux_u, COLS - 1, 1))
-        west = jnp.where(is_w, halo, pltpu.roll(flux_u, 1, 1))
-        north = jnp.where(is_n, seam_rows[1, k : k + 1, :], pltpu.roll(flux_v, ROWS - 1, 0))
-        south = jnp.where(is_s, seam_rows[4, k : k + 1, :], pltpu.roll(flux_v, 1, 0))
-        new_th[k] = th[k] - half * ((east - west) + (north - south))
+        flux_v_pad[k, 7:8, :] = seam_rows[4, k : k + 1, :]
+        flux_v_pad[k, 8 + ROWS : 9 + ROWS, :] = seam_rows[1, k : k + 1, :]
+        for begin in range(0, ROWS, 32):
+            at = slice(begin, begin + 32)
+            w = weight[k, at, :]
+            mask = levels[at] > k
+            rest_u = tail_u[k, at, :] + base_u[at] + jnp.where(is_edge, roll(pair_fix[at], shift, 1), 0.0)
+            rest_v = tail_v[k, at, :] + base_v[at]
+            if begin == 0:
+                rest_v = rest_v + jnp.where(rows16 == 0, seam_rows[3, k : k + 1, :], 0.0)
+            if begin == ROWS - 32:
+                rest_v = rest_v + jnp.where(rows16 == 32 - 1, seam_rows[0, k : k + 1, :], 0.0)
+            out_u = jnp.where(mask, rest_u, 0.0)
+            out_v = jnp.where(mask, rest_v, 0.0)
+            new_u[k, at, :] = out_u
+            new_v[k, at, :] = out_v
+            flux_u = w * out_u
+            flux_v_pad[k, 8 + begin : 8 + begin + 32, :] = w * out_v
+            halo = roll(pair_flux[at], shift, 1)
+            east = jnp.where(is_e, halo, pltpu.roll(flux_u, COLS - 1, 1))
+            west = jnp.where(is_w, halo, pltpu.roll(flux_u, 1, 1))
+            new_th[k, at, :] = th[k, at, :] - half * (east - west)
+        north = flux_v_pad[k, 9 : 9 + ROWS, :]
+        south = flux_v_pad[k, 7 : 7 + ROWS, :]
+        new_th[k] = new_th[k] - half * (north - south)
         for part, (begin, end) in enumerate(parts):
             if k == end - 1:
                 rows = pl.ds(begin, end - begin)
@@ -578,6 +597,7 @@
             held,
             held,
             held,
+            pltpu.VMEM((LAYERS, ROWS + 16, COLS), jnp.float32),
             pltpu.VMEM((3, ROWS, COLS), jnp.float32),
             pltpu.SemaphoreType.DMA((3, 4)),
             pltpu.SemaphoreType.DMA((3,)),

time: 25.4 us -> 25.4 us (level); the launches traced: 25.2 us -> 25 us
  Pallas kernels: 6.74 us -> 6.48 us
    pallas_call x1, Pallas kernels: 4.07 us -> 3.81 us  [local(): pl.pallas_call(third_kernel, out_shape=(layers, layers, layers, plane, pl...]
where the time goes in v2:
time: 25.4 us; the launch traced here: 25 us
  starting transfers between devices  10.2 us (40%)
  waiting for transfers between devices  6.76 us (27%)
  Pallas kernels  6.48 us (26%)
  between operations  0.89 us (4%)
  local copies, waits for them, and re-layouts  0.66 us (3%)
    ppermute x1, starting transfers between devices, local(): lax.ppermute(msg_b, 'lon', [(i, ((i + 1 ^ 1) - 1) % lons) for i in range(...  8.01 us
    ppermute x1, waiting for transfers between devices, exchange(): return lambda x: lax.ppermute(x, ('lon', 'lat'), pairs)  5.41 us
    pallas_call x1, Pallas kernels, local(): pl.pallas_call(third_kernel, out_shape=(layers, layers, layers, plane, pl...  3.81 us
    pallas_call x1, Pallas kernels, local(): pl.pallas_call(first_kernel, out_shape=(lon_msg, lon_msg, plane, f32(16,...  2.18 us
    ppermute x1, waiting for transfers between devices, local(): lax.ppermute(msg_b, 'lon', [(i, ((i + 1 ^ 1) - 1) % lons) for i in range(...  1.35 us
    ppermute x1, starting transfers between devices, exchange(): return lambda x: lax.ppermute(x, ('lon', 'lat'), pairs)  1.25 us
    ppermute x1, starting transfers between devices, local(): got_x = lax.ppermute(msg_x, 'lat', [(i, i ^ 1) for i in range(lats)])  0.92 us
    unnamed x2, local copies, waits for them, and re-layouts  0.66 us
  transfers between devices with their start and end apart: 4, of which 2 were waited for; matrix products, arithmetic and copies ran while one was open for 0% of the time, Pallas kernels for 0%

profile of v2, /device:TPU:6, one launch (start us, length us, event | category | flops | bytes accessed | tf_op | source)
XLA Modules:
  0.0 25.0 jit_solution(15804449130360913873)
XLA Ops:
  0.6 2.2 %edges.1 = (f32[152,128]{1,0:T(8,128)S(1)}, f32[152,128]{1,0:T(8,128)S(1)}, f32[64,128]{1,0:T(8,128)S(1)}, f32[16,128]{1,0:T(8,128)S(1)}, f32[8,64,128]{2,1,0:T(...) custom-call(f32[12]{0:T(128)} %gravity_hbm.1, ...), custom_call_target="tpu_custom_call" | custom-call | tf_op jit(solution)/shard_map/edges/pallas_call | solution.py:533
  2.8 8.0 %collective-permute-start.33 = (f32[152,128]{1,0:T(8,128)S(1)}, f32[152,128]{1,0:T(8,128)S(1)}, u32[]{:S(2)}, u32[]{:S(2)}) collective-permute-start(f32[152,128]{1,0:T(8,128)S(1)} %get-tuple-element.104), channel_id=1, source_target_pairs={{0,248},{8,16},{16,8},{24,32},{32,24},{40,48},{48,40},{56,64},{64,... | collective-permute-start | bytes 233480 | tf_op jit(solution)/shard_map/ppermute | solution.py:554
  10.8 0.0 collective-permute-start.32
  10.8 0.0 copy-start
  10.8 0.7 %copy-done = s32[128]{0:T(128)S(1)} copy-done((s32[128]{0:T(128)S(1)}, s32[128]{0:T(128)}, u32[]{:S(2)}) %copy-start) | copy-done | bytes 536
  11.6 1.3 %collective-permute-done.33.got_b = f32[152,128]{1,0:T(8,128)S(1)} collective-permute-done((f32[152,128]{1,0:T(8,128)S(1)}, f32[152,128]{1,0:T(8,128)S(1)}, u32[]{:S(2)}, u32[]{:S(2)}) %collective-permute-start.33) | collective-permute-done | bytes 77856 | tf_op jit(solution)/shard_map/ppermute | solution.py:554
  12.9 0.0 collective-permute-done.32.got_a
  12.9 0.5 %extend.1 = (f32[6,64,256]{2,1,0:T(8,128)S(1)}, f32[3,64,128]{2,1,0:T(8,128)S(1)}, f32[160,128]{1,0:T(8,128)S(1)}, f32[160,128]{1,0:T(8,128)S(1)}, f32[160,128]{1,0:T(8,128)S(1)}) custom-call(f32[16,128]{1,0:T(8,128)S(1)} %get-tuple-element.92.g_rows, f32[128,128]{1,0:T(8,128)S(1)} %get-tuple-element.100.to_potential, ...), custom_call_target="tpu_custom_call" | custom-call | tf_op jit(solution)/shard_map/extend/pallas_call | solution.py:557
  13.4 0.9 %collective-permute-start.34 = (f32[160,128]{1,0:T(8,128)S(1)}, f32[160,128]{1,0:T(8,128)S(1)}, u32[]{:S(2)}, u32[]{:S(2)}) collective-permute-start(f32[160,128]{1,0:T(8,128)S(1)} %get-tuple-element.109.own_x), channel_id=1, source_target_pairs={{0,1},{1,0},{2,3},{3,2},{4,5},{5,4},{6,7},{7,6},{8,9},{9,8},{10,11... | collective-permute-start | bytes 245768 | tf_op jit(solution)/shard_map/ppermute | solution.py:566
  14.3 6.7 %conditional.1 = (f32[160,128]{1,0:T(8,128)}) conditional(s32[]{:T(128)} %clamp.3, f32[160,128]{1,0:T(8,128)S(1)} %get-tuple-element.111.own_f, f32[160,128]{1,0:T(8,128)S(1)} %get-tuple-element.111.own_f, f32[160,128]{1,0:T(8,128)S(1)} %get-tuple-element.111.own_f, ...), branch_computations={%region_0.1_spmd, %region_1.2_spmd, %region_2.3_spmd, %region_3.4_... | conditional | bytes 327728 | solution.py:579
  14.3 1.2 %collective-permute-start.14 = (f32[160,128]{1,0:T(8,128)S(1)}, f32[160,128]{1,0:T(8,128)}, u32[]{:S(2)}, u32[]{:S(2)}) collective-permute-start(f32[160,128]{1,0:T(8,128)S(1)} %param.14), channel_id=1, source_target_pairs={{1,2},{2,1},{3,4},{4,3},{5,6},{6,5},{9,10},{10,9},{11,12},{12,11},... | collective-permute-start | bytes 245768 | tf_op jit(solution)/shard_map/cond/branch_14_fun/ppermute | solution.py:577
  15.6 5.4 %collective-permute-done.14 = f32[160,128]{1,0:T(8,128)} collective-permute-done((f32[160,128]{1,0:T(8,128)S(1)}, f32[160,128]{1,0:T(8,128)}, u32[]{:S(2)}, u32[]{:S(2)}) %collective-permute-start.14) | collective-permute-done | bytes 81952 | tf_op jit(solution)/shard_map/cond/branch_14_fun/ppermute | solution.py:577
  21.0 0.0 collective-permute-done.34.got_x
  21.0 3.8 %advance.1 = (f32[12,64,128]{2,1,0:T(8,128)}, f32[12,64,128]{2,1,0:T(8,128)}, f32[12,64,128]{2,1,0:T(8,128)}, f32[64,128]{1,0:T(8,128)}, f32[64,128]{1,0:T(8,128)}, /*index=5*/f32[64,128]{1,0:T(8,128)}) custom-call(f32[16,128]{1,0:T(8,128)S(1)} %get-tuple-element.92.g_rows, f32[12,64,128]{2,1,0:T(8,128)S(1)} %get-tuple-element.93.tail_u, ...), custom_call_target="tpu_custom_call" | custom-call | tf_op jit(solution)/shard_map/advance/pallas_call | solution.py:583
Async XLA Ops:
  2.8 10.1 %collective-permute-start.33 = (f32[152,128]{1,0:T(8,128)S(1)}, f32[152,128]{1,0:T(8,128)S(1)}, u32[]{:S(2)}, u32[]{:S(2)}) collective-permute-start(f32[152,128]{1,0:T(8,128)S(1)} %get-tuple-element.104), channel_id=1, source_target_pairs={{0,248},{8,16},{16,8},{24,32},{32,24},{40,48},{48,40},{56,64},{64,... | collective-permute-start | bytes 233480 | tf_op jit(solution)/shard_map/ppermute | solution.py:554
  10.8 2.1 %collective-permute-start.32 = (f32[152,128]{1,0:T(8,128)S(1)}, f32[152,128]{1,0:T(8,128)S(1)}, u32[]{:S(2)}, u32[]{:S(2)}) collective-permute-start(f32[152,128]{1,0:T(8,128)S(1)} %get-tuple-element.103.own_a), channel_id=1, source_target_pairs={{0,8},{8,0},{16,24},{24,16},{32,40},{40,32},{48,56},{56,48},{64,72... | collective-permute-start | bytes 233480 | tf_op jit(solution)/shard_map/ppermute | solution.py:553
  10.8 0.7 %copy-start = (s32[128]{0:T(128)S(1)}, s32[128]{0:T(128)}, u32[]{:S(2)}) copy-start(s32[128]{0:T(128)} %fold_hbm.1) | copy-start | bytes 1540
  13.4 7.6 %collective-permute-start.34 = (f32[160,128]{1,0:T(8,128)S(1)}, f32[160,128]{1,0:T(8,128)S(1)}, u32[]{:S(2)}, u32[]{:S(2)}) collective-permute-start(f32[160,128]{1,0:T(8,128)S(1)} %get-tuple-element.109.own_x), channel_id=1, source_target_pairs={{0,1},{1,0},{2,3},{3,2},{4,5},{5,4},{6,7},{7,6},{8,9},{9,8},{10,11... | collective-permute-start | bytes 245768 | tf_op jit(solution)/shard_map/ppermute | solution.py:566
  14.3 6.7 %collective-permute-start.14 = (f32[160,128]{1,0:T(8,128)S(1)}, f32[160,128]{1,0:T(8,128)}, u32[]{:S(2)}, u32[]{:S(2)}) collective-permute-start(f32[160,128]{1,0:T(8,128)S(1)} %param.14), channel_id=1, source_target_pairs={{1,2},{2,1},{3,4},{4,3},{5,6},{6,5},{9,10},{10,9},{11,12},{12,11},... | collective-permute-start | bytes 245768 | tf_op jit(solution)/shard_map/cond/branch_14_fun/ppermute | solution.py:577

commit v3 on v2

--- a/solution.py
+++ b/solution.py
@@ -217,6 +217,14 @@
     lane12 = lane_index((LAYERS, COLS))
     lane16 = lane_index((HALO, COLS))
 
+    def weight_rows(msg, w_at):
+        msg[LAT_W : LAT_W + LAYERS, :] = own_a[w_at : w_at + LAYERS, :]
+        beside_e = jnp.where(even_lon, got_a[w_at : w_at + LAYERS, :], got_b[w_at : w_at + LAYERS, :])
+        beside_w = jnp.where(even_lon, got_b[w_at : w_at + LAYERS, :], got_a[w_at : w_at + LAYERS, :])
+        beside = roll(jnp.where(lane12 < HALO, beside_e, beside_w), HALO + 64, 1)
+        held = msg[LAT_SIDE + HALO : LAT_SIDE + HALO + LAYERS, :]
+        msg[LAT_SIDE + HALO : LAT_SIDE + HALO + LAYERS, :] = jnp.where(lane12 // 32 == 2, beside, held)
+
     def lat_message(msg, north):
         start, w_at = (ROWS - HALO, W_TOP) if north else (0, W_BOTTOM)
         edge, c_at, v_at = (own_a, C_TOP, V_TOP) if north else (own_rows, 0, V_BOTTOM)
@@ -227,28 +235,30 @@
             packed[f // 4] = jnp.where(lane16 // 32 == f % 4, side, packed[f // 4])
         msg[LAT_SIDE : LAT_SIDE + HALO, :] = packed[0]
         msg[LAT_SIDE + HALO :, :] = packed[1]
-        msg[LAT_W : LAT_W + LAYERS, :] = own_a[w_at : w_at + LAYERS, :]
-        beside_e = jnp.where(even_lon, got_a[w_at : w_at + LAYERS, :], got_b[w_at : w_at + LAYERS, :])
-        beside_w = jnp.where(even_lon, got_b[w_at : w_at + LAYERS, :], got_a[w_at : w_at + LAYERS, :])
-        beside = roll(jnp.where(lane12 < HALO, beside_e, beside_w), HALO + 64, 1)
-        held = msg[LAT_SIDE + HALO : LAT_SIDE + HALO + LAYERS, :]
-        msg[LAT_SIDE + HALO : LAT_SIDE + HALO + LAYERS, :] = jnp.where(lane12 // 32 == 2, beside, held)
+        weight_rows(msg, w_at)
         msg[LAT_C : LAT_C + LAYERS, :] = edge[c_at : c_at + LAYERS, :]
         msg[LAT_V : LAT_V + 1, :] = edge[v_at : v_at + 1, :]
         msg[LAT_V + 1 : LAT_SIDE, :] = jnp.zeros((LAT_SIDE - LAT_V - 1, COLS), jnp.float32)
 
+    at_top = lat == lax.axis_size("lat") - 1
+    msg_y[LAT_SIDE + HALO :, :] = jnp.zeros((HALO, COLS), jnp.float32)
+
     @pl.when(even_lat)
     def _():
         lat_message(msg_x, True)
-        lat_message(msg_y, False)
+        lat_message(msg_f, False)
+        weight_rows(msg_y, W_BOTTOM)
 
     @pl.when(jnp.logical_not(even_lat))
     def _():
         lat_message(msg_x, False)
-        lat_message(msg_y, True)
-
-
-    @pl.when(lat == lax.axis_size("lat") - 1)
+        weight_rows(msg_y, W_TOP)
+
+    @pl.when(jnp.logical_not(even_lat) & jnp.logical_not(at_top))
+    def _():
+        lat_message(msg_f, True)
+
+    @pl.when(at_top)
     def _():
         lane8 = lane_index((8, COLS))
         row8 = row_index((8, COLS))
@@ -299,10 +309,6 @@
         msg_f[LAT_V : LAT_V + 8, :] = -main
         for at, x in packed.items():
             msg_f[at : at + 8, :] = x
-
-    @pl.when(lat != lax.axis_size("lat") - 1)
-    def _():
-        msg_f[...] = msg_y[...]
 
 
 def third_kernel(
@@ -550,8 +556,8 @@
         name="edges",
     )(*in_hbm(gravity, lu, lv, th, lev, u, v, land, bottom, fold_map))
 
+    got_b = lax.ppermute(msg_b, "lon", [(i, (((i + 1) ^ 1) - 1) % lons) for i in range(lons)])
     got_a = lax.ppermute(msg_a, "lon", [(i, i ^ 1) for i in range(lons)])
-    got_b = lax.ppermute(msg_b, "lon", [(i, (((i + 1) ^ 1) - 1) % lons) for i in range(lons)])
     got_a, got_b, shift = lax.optimization_barrier((got_a, got_b, shift))
 
     ext, edges, msg_x, msg_y, msg_f = pl.pallas_call(

time: 25.4 us -> 25.2 us (level)
  no operation moved by 1% of the time
where the time goes in v3:
time: 25.2 us; the launch traced here: 25 us
  starting transfers between devices  10.2 us (40%)
  waiting for transfers between devices  6.7 us (27%)
  Pallas kernels  6.54 us (26%)
  between operations  0.89 us (4%)
  local copies, waits for them, and re-layouts  0.66 us (3%)
    ppermute x1, starting transfers between devices, local(): lax.ppermute(msg_b, 'lon', [(i, ((i + 1 ^ 1) - 1) % lons) for i in range(...  8.01 us
    ppermute x1, waiting for transfers between devices, exchange(): return lambda x: lax.ppermute(x, ('lon', 'lat'), pairs)  5.34 us
    pallas_call x1, Pallas kernels, local(): pl.pallas_call(third_kernel, out_shape=(layers, layers, layers, plane, pl...  3.81 us
    pallas_call x1, Pallas kernels, local(): pl.pallas_call(first_kernel, out_shape=(lon_msg, lon_msg, plane, f32(16,...  2.18 us
    ppermute x1, waiting for transfers between devices, local(): lax.ppermute(msg_b, 'lon', [(i, ((i + 1 ^ 1) - 1) % lons) for i in range(...  1.35 us
    ppermute x1, starting transfers between devices, exchange(): return lambda x: lax.ppermute(x, ('lon', 'lat'), pairs)  1.31 us
    ppermute x1, starting transfers between devices, local(): got_x = lax.ppermute(msg_x, 'lat', [(i, i ^ 1) for i in range(lats)])  0.86 us
    unnamed x2, local copies, waits for them, and re-layouts  0.66 us
  transfers between devices with their start and end apart: 4, of which 2 were waited for; matrix products, arithmetic and copies ran while one was open for 0% of the time, Pallas kernels for 0%

profile of v3, /device:TPU:6, one launch (start us, length us, event | category | flops | bytes accessed | tf_op | source)
XLA Modules:
  0.0 25.0 jit_solution(10704620544054236183)
XLA Ops:
  0.6 2.2 %edges.1 = (f32[152,128]{1,0:T(8,128)S(1)}, f32[152,128]{1,0:T(8,128)S(1)}, f32[64,128]{1,0:T(8,128)S(1)}, f32[16,128]{1,0:T(8,128)S(1)}, f32[8,64,128]{2,1,0:T(...) custom-call(f32[12]{0:T(128)} %gravity_hbm.1, ...), custom_call_target="tpu_custom_call" | custom-call | tf_op jit(solution)/shard_map/edges/pallas_call | solution.py:539
  2.8 8.0 %collective-permute-start.33 = (f32[152,128]{1,0:T(8,128)S(1)}, f32[152,128]{1,0:T(8,128)S(1)}, u32[]{:S(2)}, u32[]{:S(2)}) collective-permute-start(f32[152,128]{1,0:T(8,128)S(1)} %get-tuple-element.104), channel_id=1, source_target_pairs={{0,248},{8,16},{16,8},{24,32},{32,24},{40,48},{48,40},{56,64},{64,... | collective-permute-start | bytes 233480 | tf_op jit(solution)/shard_map/ppermute | solution.py:559
  10.8 0.0 collective-permute-start.32
  10.8 0.0 copy-start
  10.8 0.7 %copy-done = s32[128]{0:T(128)S(1)} copy-done((s32[128]{0:T(128)S(1)}, s32[128]{0:T(128)}, u32[]{:S(2)}) %copy-start) | copy-done | bytes 536
  11.6 1.3 %collective-permute-done.33.got_b = f32[152,128]{1,0:T(8,128)S(1)} collective-permute-done((f32[152,128]{1,0:T(8,128)S(1)}, f32[152,128]{1,0:T(8,128)S(1)}, u32[]{:S(2)}, u32[]{:S(2)}) %collective-permute-start.33) | collective-permute-done | bytes 77856 | tf_op jit(solution)/shard_map/ppermute | solution.py:559
  12.9 0.0 collective-permute-done.32.got_a
  12.9 0.6 %extend.1 = (f32[6,64,256]{2,1,0:T(8,128)S(1)}, f32[3,64,128]{2,1,0:T(8,128)S(1)}, f32[160,128]{1,0:T(8,128)S(1)}, f32[160,128]{1,0:T(8,128)S(1)}, f32[160,128]{1,0:T(8,128)S(1)}) custom-call(f32[16,128]{1,0:T(8,128)S(1)} %get-tuple-element.92.g_rows, f32[128,128]{1,0:T(8,128)S(1)} %get-tuple-element.100.to_potential, ...), custom_call_target="tpu_custom_call" | custom-call | tf_op jit(solution)/shard_map/extend/pallas_call | solution.py:563
  13.5 0.9 %collective-permute-start.34 = (f32[160,128]{1,0:T(8,128)S(1)}, f32[160,128]{1,0:T(8,128)S(1)}, u32[]{:S(2)}, u32[]{:S(2)}) collective-permute-start(f32[160,128]{1,0:T(8,128)S(1)} %get-tuple-element.109.own_x), channel_id=1, source_target_pairs={{0,1},{1,0},{2,3},{3,2},{4,5},{5,4},{6,7},{7,6},{8,9},{9,8},{10,11... | collective-permute-start | bytes 245768 | tf_op jit(solution)/shard_map/ppermute | solution.py:572
  14.3 6.7 %conditional.1 = (f32[160,128]{1,0:T(8,128)}) conditional(s32[]{:T(128)} %clamp.3, f32[160,128]{1,0:T(8,128)S(1)} %get-tuple-element.111.own_f, f32[160,128]{1,0:T(8,128)S(1)} %get-tuple-element.111.own_f, f32[160,128]{1,0:T(8,128)S(1)} %get-tuple-element.111.own_f, ...), branch_computations={%region_0.1_spmd, %region_1.2_spmd, %region_2.3_spmd, %region_3.4_... | conditional | bytes 327728 | solution.py:585
  14.3 1.3 %collective-permute-start.4 = (f32[160,128]{1,0:T(8,128)S(1)}, f32[160,128]{1,0:T(8,128)}, u32[]{:S(2)}, u32[]{:S(2)}) collective-permute-start(f32[160,128]{1,0:T(8,128)S(1)} %param.4), channel_id=1, source_target_pairs={{1,2},{2,1},{3,4},{4,3},{5,6},{6,5},{9,10},{10,9},{11,12},{12,11},... | collective-permute-start | bytes 245768 | tf_op jit(solution)/shard_map/cond/branch_4_fun/ppermute | solution.py:583
  15.6 5.3 %collective-permute-done.4 = f32[160,128]{1,0:T(8,128)} collective-permute-done((f32[160,128]{1,0:T(8,128)S(1)}, f32[160,128]{1,0:T(8,128)}, u32[]{:S(2)}, u32[]{:S(2)}) %collective-permute-start.4) | collective-permute-done | bytes 81952 | tf_op jit(solution)/shard_map/cond/branch_4_fun/ppermute | solution.py:583
  21.0 0.0 collective-permute-done.34.got_x
  21.0 3.8 %advance.1 = (f32[12,64,128]{2,1,0:T(8,128)}, f32[12,64,128]{2,1,0:T(8,128)}, f32[12,64,128]{2,1,0:T(8,128)}, f32[64,128]{1,0:T(8,128)}, f32[64,128]{1,0:T(8,128)}, /*index=5*/f32[64,128]{1,0:T(8,128)}) custom-call(f32[16,128]{1,0:T(8,128)S(1)} %get-tuple-element.92.g_rows, f32[12,64,128]{2,1,0:T(8,128)S(1)} %get-tuple-element.93.tail_u, ...), custom_call_target="tpu_custom_call" | custom-call | tf_op jit(solution)/shard_map/advance/pallas_call | solution.py:589
Async XLA Ops:
  2.8 10.1 %collective-permute-start.33 = (f32[152,128]{1,0:T(8,128)S(1)}, f32[152,128]{1,0:T(8,128)S(1)}, u32[]{:S(2)}, u32[]{:S(2)}) collective-permute-start(f32[152,128]{1,0:T(8,128)S(1)} %get-tuple-element.104), channel_id=1, source_target_pairs={{0,248},{8,16},{16,8},{24,32},{32,24},{40,48},{48,40},{56,64},{64,... | collective-permute-start | bytes 233480 | tf_op jit(solution)/shard_map/ppermute | solution.py:559
  10.8 2.1 %collective-permute-start.32 = (f32[152,128]{1,0:T(8,128)S(1)}, f32[152,128]{1,0:T(8,128)S(1)}, u32[]{:S(2)}, u32[]{:S(2)}) collective-permute-start(f32[152,128]{1,0:T(8,128)S(1)} %get-tuple-element.103.own_a), channel_id=1, source_target_pairs={{0,8},{8,0},{16,24},{24,16},{32,40},{40,32},{48,56},{56,48},{64,72... | collective-permute-start | bytes 233480 | tf_op jit(solution)/shard_map/ppermute | solution.py:560
  10.8 0.7 %copy-start = (s32[128]{0:T(128)S(1)}, s32[128]{0:T(128)}, u32[]{:S(2)}) copy-start(s32[128]{0:T(128)} %fold_hbm.1) | copy-start | bytes 1540
  13.5 7.5 %collective-permute-start.34 = (f32[160,128]{1,0:T(8,128)S(1)}, f32[160,128]{1,0:T(8,128)S(1)}, u32[]{:S(2)}, u32[]{:S(2)}) collective-permute-start(f32[160,128]{1,0:T(8,128)S(1)} %get-tuple-element.109.own_x), channel_id=1, source_target_pairs={{0,1},{1,0},{2,3},{3,2},{4,5},{5,4},{6,7},{7,6},{8,9},{9,8},{10,11... | collective-permute-start | bytes 245768 | tf_op jit(solution)/shard_map/ppermute | solution.py:572
  14.3 6.7 %collective-permute-start.4 = (f32[160,128]{1,0:T(8,128)S(1)}, f32[160,128]{1,0:T(8,128)}, u32[]{:S(2)}, u32[]{:S(2)}) collective-permute-start(f32[160,128]{1,0:T(8,128)S(1)} %param.4), channel_id=1, source_target_pairs={{1,2},{2,1},{3,4},{4,3},{5,6},{6,5},{9,10},{10,9},{11,12},{12,11},... | collective-permute-start | bytes 245768 | tf_op jit(solution)/shard_map/cond/branch_4_fun/ppermute | solution.py:583
